TPU v7x, 32 devices: a whole 2x2x4 slice. The times are simulated.
32 devices in a mesh: dp: 16 (over z, y, x), tp: 2 (over core).
Axes of the slice: x: 2, y: 2, z: 4, core: 2. Of those that a mesh axis runs over, the one named last changes fastest.
Arguments:
- images: float32 [192, 197, 384], P('dp'), may hold values from -6 to 6
- image_count: int32 [16], P('dp'), may hold values from 3 to 12, as said below
- cotangent: float32 [192, 197, 384], P('dp'), may hold values from -6 to 6
- w_query: float32 [384, 384], P('dp', 'tp'), may hold values from -0.3125 to 0.3125
- w_key: float32 [384, 384], P('dp', 'tp'), may hold values from -0.3125 to 0.3125
- w_value: float32 [384, 384], P('dp', 'tp'), may hold values from -0.3125 to 0.3125
- w_out: float32 [384, 384], P('tp', 'dp'), may hold values from -2 to 2
- w_up: float32 [384, 1536], P('dp', 'tp'), may hold values from -0.3125 to 0.3125
- w_down: float32 [1536, 384], P('tp', 'dp'), may hold values from -0.15625 to 0.15625
- vectors: float32 [4608], P(('dp', 'tp')), may hold values from -0.9 to 1.4
- mom_query: float32 [384, 384], P('dp', 'tp'), may hold values from -320 to 320
- mom_key: float32 [384, 384], P('dp', 'tp'), may hold values from -320 to 320
- mom_value: float32 [384, 384], P('dp', 'tp'), may hold values from -320 to 320
- mom_out: float32 [384, 384], P('tp', 'dp'), may hold values from -320 to 320
- mom_up: float32 [384, 1536], P('dp', 'tp'), may hold values from -320 to 320
- mom_down: float32 [1536, 384], P('tp', 'dp'), may hold values from -320 to 320
- adam_first: float32 [4608], P(('dp', 'tp')), may hold values from -96 to 96
- adam_second: float32 [4608], P(('dp', 'tp')), may hold values from 7.5648 to 75.648
Outputs:
- block_out: float32 [192, 197, 384], P('dp')
- input_grad: float32 [192, 197, 384], P('dp')
- grad_query: float32 [384, 384], P('dp', 'tp')
- grad_key: float32 [384, 384], P('dp', 'tp')
- grad_value: float32 [384, 384], P('dp', 'tp')
- grad_out: float32 [384, 384], P('tp', 'dp')
- grad_up: float32 [384, 1536], P('dp', 'tp')
- grad_down: float32 [1536, 384], P('tp', 'dp')
- grad_vectors: float32 [4608], P(('dp', 'tp'))
- new_mom_query: float32 [384, 384], P('dp', 'tp')
- new_mom_key: float32 [384, 384], P('dp', 'tp')
- new_mom_value: float32 [384, 384], P('dp', 'tp')
- new_mom_out: float32 [384, 384], P('tp', 'dp')
- new_mom_up: float32 [384, 1536], P('dp', 'tp')
- new_mom_down: float32 [1536, 384], P('tp', 'dp')
- step_query: float32 [384, 384], P('dp', 'tp')
- step_key: float32 [384, 384], P('dp', 'tp')
- step_value: float32 [384, 384], P('dp', 'tp')
- step_out: float32 [384, 384], P('tp', 'dp')
- step_up: float32 [384, 1536], P('dp', 'tp')
- step_down: float32 [1536, 384], P('tp', 'dp')
- first_new: float32 [4608], P(('dp', 'tp'))
- second_new: float32 [4608], P(('dp', 'tp'))
- vector_update: float32 [4608], P(('dp', 'tp'))
Inputs may be any that keep to these rules, and one draw needn't show every extreme that they name: `image_count`: each index of dp holds between max(1, 12 div 4) and 12 live images; some index holds 12 and some the least.
All inputs are finite; a program needn't handle non-finite values.
Results may differ from a plain program's by a relative error of at most 0.0003.
Values sent between devices are 32-bit elements; how exact they have to be, the bound alone decides.
No kernel may reach another device: no remote copies, remote signals or barrier semaphores. Data moves between devices by JAX's collectives and lax.ppermute only.
A program may use at most 256 MiB of HBM per device.

v0:
```python
import functools
import math

import jax
import jax.numpy as jnp
import numpy as np
from jax import lax
from jax.experimental import pallas as pl
from jax.experimental.pallas import tpu as pltpu
from jax.sharding import PartitionSpec as P

D = 384
HEADS = 6
HEAD_DIM = 64
FF = 1536
SEQ = 197
PAD = 208
GROUP = 2
COLUMNS = 256
PARTS = 3
UNROLL = 3
NS_STEPS = 5
STEP = 10
HALF = D // 2
SLOTS = 4
VEC = 4608
UNITS = FF // 2

norm_eps = 1e-06
ns_first = 3.4445
ns_second = -4.775
ns_third = 2.0315
momentum_decay = 0.95
matrix_rate = 1.0
adam_beta_one = 0.9
adam_beta_two = 0.999
adam_rate = 0.05
adam_decay = 0.05
adam_eps = 1e-08
f32 = jnp.float32
bf16 = jnp.bfloat16
VMEM_BYTES = 60 * 2**20
ONCE = pl.Buffered(1)


def split(value):
    high = value.astype(bf16)
    return high, (value - high.astype(f32)).astype(bf16)


def dot_one(left, right, left_dim, right_dim):
    return lax.dot_general(
        left, right, (((left_dim,), (right_dim,)), ((), ())), preferred_element_type=f32
    )


def dot(left, right, left_dim, right_dim):
    left_high, left_low = left if isinstance(left, tuple) else split(left)
    right_high, right_low = right if isinstance(right, tuple) else split(right)
    return dot_one(left_high, right_high, left_dim, right_dim) + (
        dot_one(left_high, right_low, left_dim, right_dim)
        + dot_one(left_low, right_high, left_dim, right_dim)
    )


def nn(left, right):
    return dot(left, right, 1, 0)


def nt(left, right):
    return dot(left, right, 1, 1)


def tn(left, right):
    return dot(left, right, 0, 0)


def levels(dp_size):
    bits = dp_size.bit_length() - 1
    out = []
    shift = 0
    while bits:
        width = min(2, bits)
        out.append((shift, 1 << width))
        shift += width
        bits -= width
    return out[::-1]


def padded_rows(dp_size):
    return -(-(D // dp_size) // 8) * 8


def swap_dp(value, mask, dp_size):
    return lax.ppermute(value, "dp", [(i, i ^ mask) for i in range(dp_size)])


def swap_tp(value):
    return lax.ppermute(value, "tp", [(0, 1), (1, 0)])


def tie(first, second):
    return lax.optimization_barrier((first, second))


def exchange(block, level, dp_size):
    shift, size = level
    return [swap_dp(block, s << shift, dp_size) for s in range(1, size)]


def gather(block, groups, dp_size):
    for level in groups:
        block = jnp.concatenate([block] + exchange(block, level, dp_size), axis=0)
    return block


def place_of(value, groups):
    place = 0
    stride = 1
    for shift, size in groups:
        place = place + ((value >> shift) & (size - 1)) * stride
        stride *= size
    return place


def scatter_sum(value, groups, dp_size):
    for shift, size in groups[::-1]:
        value = value.reshape((size, -1) + value.shape[1:])
        total = value[0]
        for part in [swap_dp(value[s], s << shift, dp_size) for s in range(1, size)]:
            total = total + part
        value = total
    return value


def normalize(rows):
    centre = jnp.sum(rows, axis=-1, keepdims=True) * (1.0 / D)
    offset = rows - centre
    spread = jnp.sum(offset * offset, axis=-1, keepdims=True) * (1.0 / D)
    rate = lax.rsqrt(spread + norm_eps)
    return offset * rate, rate


def normalize_back(grad, unit, rate, gain):
    scaled = grad * gain
    mean_one = jnp.sum(scaled, axis=-1, keepdims=True) * (1.0 / D)
    mean_two = jnp.sum(scaled * unit, axis=-1, keepdims=True) * (1.0 / D)
    return rate * (scaled - mean_one - unit * mean_two)


def row_sum(value):
    return jnp.sum(value, axis=0, keepdims=True)


def lanes(*parts):
    return jnp.concatenate(parts, axis=1)


def lines(*parts):
    return jnp.concatenate(parts, axis=0)


def left_three(value):
    high, low = split(value)
    return lanes(high, high, low)


def weights_three(value):
    high, low = split(value)
    return lines(high, low, high)


def rows_left(value):
    high, low = split(value)
    return lines(high, high, low)


def rows_right(value):
    high, low = split(value)
    return lines(high, low, high)


def nt_wide(left, weights):
    high, low = split(left)
    count = weights.shape[0] // 2
    both = dot_one(high, weights, 1, 1)
    return both[:, :count] + (both[:, count:] + dot_one(low, weights[:count], 1, 1))


def stack_pair(value):
    lane = lax.broadcasted_iota(jnp.int32, value.shape, 1)
    gap = jnp.zeros((COLUMNS - PAD, value.shape[1]), f32)
    return lines(
        jnp.where(lane < HEAD_DIM, value, 0.0), gap, jnp.where(lane < HEAD_DIM, 0.0, value), gap
    )


def pair_product(left_high, left_low, right):
    both = dot_one(left_high, lanes(*right), 1, 0)
    width = right[0].shape[1]
    return both[:, :width] + (both[:, width:] + dot_one(left_low, right[0], 1, 0))


def relative(vec, is_first):
    half = vec.shape[1] // 2
    return jnp.where(is_first, vec, jnp.concatenate([vec[:, half:], vec[:, :half]], axis=1))


def for_plane(dp_size, info, parts, place):
    every = levels(dp_size)
    count = every[-1][1]
    for low in range(count):

        @pl.when((info[1] & (count - 1)) == low)
        def _():
            for j in range(dp_size):
                at = place_of(info[1] ^ j, every[:-1])
                place(j, *[group[(j % count) ^ low][at] for group in parts])


def attention_forward(dp_size, info, images, *rest):
    count = levels(dp_size)[-1][1]
    own, other = rest[:count], rest[count : 2 * count]
    qkv_out, att_out, hid_out, wqkv_out, wo_out, vec_out, xs, plain_w, wqkv, wo, att, vec = rest[2 * count :]
    attention_forward_body(
        dp_size, info, images, own, other, qkv_out, att_out, hid_out, wqkv_out, wo_out, vec_out, xs, plain_w, wqkv, wo, att, vec
    )


def attention_forward_body(dp_size, info, images, own, other, qkv_out, att_out, hid_out, wqkv_out, wo_out, vec_out, xs, plain_w, wqkv, wo, att, vec):
    step = pl.program_id(0)
    rows = D // dp_size
    is_first = info[0] == 0

    @pl.when(step == 0)
    def _():
        xs[...] = jnp.zeros_like(xs)
        piece = VEC // (2 * dp_size)

        def place(j, mine, theirs):
            here = slice(j * rows, (j + 1) * rows)
            for kind in range(4):
                plain_w[here, kind * D : kind * D + HALF] = mine[:, kind * HALF : (kind + 1) * HALF]
                plain_w[here, kind * D + HALF : (kind + 1) * D] = theirs[:, kind * HALF : (kind + 1) * HALF]
            for line in range(-(-piece // 128)):
                size = min(128, piece - line * 128)
                one = mine[line : line + 1, 4 * HALF : 4 * HALF + size]
                two = theirs[line : line + 1, 4 * HALF : 4 * HALF + size]
                base = 2 * j * piece + line * 128
                vec[0:1, base : base + size] = jnp.where(is_first, one, two)
                vec[0:1, base + piece : base + piece + size] = jnp.where(is_first, two, one)

        for_plane(dp_size, info, (own, other), place)
        wqkv[...] = weights_three(plain_w[:, : 3 * D])
        wo[...] = weights_three(plain_w[:, 3 * D :])

    xs[:, :SEQ, :] = images[...]
    tokens = xs[...].reshape(GROUP * PAD, D)
    unit, _ = normalize(tokens)
    normed = unit * vec[0:1, :D] + vec[0:1, 2 * D : 3 * D]
    bias = lanes(
        relative(vec[0:1, 4 * D : 5 * D], is_first),
        jnp.zeros((1, D), f32),
        relative(vec[0:1, 5 * D : 6 * D], is_first),
    )
    qkv = dot_one(left_three(normed), wqkv[...], 1, 0) + bias
    qkv_out[...] = qkv.reshape(GROUP, PAD, 3 * D)
    column = lax.broadcasted_iota(jnp.int32, (PAD, 2 * COLUMNS), 1) & (COLUMNS - 1)
    lane = lax.broadcasted_iota(jnp.int32, (PAD, 2 * HEAD_DIM), 1)

    def head_pair(index, carry):
        image = index // (HEADS // 2)
        pair = index % (HEADS // 2)

        def at(base):
            return pl.ds(pl.multiple_of(base + pair * 128, 128), 128)

        query_high, query_low = split(qkv_out[image, :, at(0)] * 0.125)
        key_high, key_low = split(stack_pair(qkv_out[image, :, at(D)]))
        value = split(stack_pair(qkv_out[image, :, at(2 * D)]))
        scores = dot_one(
            lanes(query_high, query_high, query_low), lanes(key_high, key_low, key_high), 1, 1
        )
        scores = jnp.where(column < SEQ, scores, -1e30)
        parts = []
        totals = []
        for half in (scores[:, :COLUMNS], scores[:, COLUMNS:]):
            part = jnp.exp(half - jnp.max(half, axis=-1, keepdims=True))
            parts.append(part)
            totals.append(1.0 / jnp.sum(part, axis=-1, keepdims=True))
        weights_high, weights_low = split(lanes(*parts))
        result = pair_product(weights_high, weights_low, value)
        att[pl.ds(pl.multiple_of(image * PAD, 16), PAD), at(0)] = result * jnp.where(
            lane < HEAD_DIM, totals[0], totals[1]
        )
        return carry

    lax.fori_loop(0, GROUP * HEADS // 2, head_pair, 0, unroll=UNROLL)
    attended = att[...]
    att_out[...] = attended.reshape(GROUP, PAD, D)
    hidden = tokens + nt_wide(attended, wo[: 2 * D]) + vec[0:1, 6 * D : 7 * D]
    hid_out[...] = hidden.reshape(GROUP, PAD, D)

    @pl.when(step == pl.num_programs(0) - 1)
    def _():
        wqkv_out[...] = wqkv[...]
        wo_out[...] = wo[...]
        vec_out[...] = vec[...]


def mlp(dp_size, info, hid, att, cot, *rest):
    count = levels(dp_size)[-1][1]
    own, other, (wo, vec) = rest[:count], rest[count : 2 * count], rest[2 * count : 2 * count + 2]
    block_out, dh_out, datt_out, *more = rest[2 * count + 2 :]
    keeps, sends, more = more[:SLOTS], more[SLOTS : 2 * SLOTS], more[2 * SLOTS :]
    mlp_body(
        dp_size, info, hid, att, cot, own, other, wo, vec, block_out, dh_out, datt_out, keeps, sends, *more
    )


def mlp_body(dp_size, info, hid, att, cot, own, other, wo, vec, block_out, dh_out, datt_out, keeps, sends, gout_out, sums, wup, wdown, cs, gup, gdown, gout, second_lanes, dy_lanes, second_rows, dy_rows, result, dsecond, bias):
    step = pl.program_id(0)
    rows = D // dp_size

    @pl.when(step == 0)
    def _():
        cs[...] = jnp.zeros_like(cs)

        def place(j, mine, theirs):
            here = slice(j * rows, (j + 1) * rows)
            gup[here, :UNITS] = mine[:, :UNITS]
            gup[here, UNITS:] = theirs[:, :UNITS]
            gdown[here, :UNITS] = mine[:, UNITS:]
            gdown[here, UNITS:] = theirs[:, UNITS:]

        for_plane(dp_size, info, (own, other), place)
        wup[...] = weights_three(gup[...])
        wdown[...] = weights_three(gdown[...])
        gup[...] = jnp.zeros_like(gup)
        gdown[...] = jnp.zeros_like(gdown)
        gout[...] = jnp.zeros_like(gout)
        sums[...] = jnp.zeros_like(sums)

    first = (info[0] * pl.num_programs(0) + step) * GROUP
    lives = [jnp.where(first + image < info[2], 1.0, 0.0).astype(f32) for image in range(GROUP)]
    for image in range(GROUP):
        cs[image, :SEQ, :] = cot[image] * lives[image]
    hidden = hid[...].reshape(GROUP * PAD, D)
    unit, rate = normalize(hidden)
    gain = vec[0:1, D : 2 * D]
    second = unit * gain + vec[0:1, 3 * D : 4 * D]
    dy = cs[...].reshape(GROUP * PAD, D)
    bias[...] = relative(vec[0:1, 8 * D :], info[0] == 0)
    second_lanes[...] = left_three(second)
    second_rows[...] = rows_left(second)
    dy_lanes[...] = left_three(dy)
    dy_rows[...] = rows_left(dy)
    result[...] = hidden + vec[0:1, 7 * D : 8 * D]
    dsecond[...] = jnp.zeros_like(dsecond)

    def units(part, carry):
        width = FF // PARTS
        here = pl.ds(pl.multiple_of(part * width, 128), width)
        pre = dot_one(second_lanes[...], wup[:, here], 1, 0) + bias[:, here]
        dact = dot_one(dy_lanes[...], wdown[:, here], 1, 0)
        phi = 0.5 * (1.0 + lax.erf(pre * math.sqrt(0.5)))
        slope = phi + pre * (jnp.exp(-0.5 * pre * pre) * (1.0 / math.sqrt(2.0 * math.pi)))
        act = pre * phi
        dpre = dact * slope
        result[...] += nt_wide(act, wdown[: 2 * D, here])
        gdown[:, here] += dot_one(dy_rows[...], rows_right(act), 0, 0)
        gup[:, here] += dot_one(second_rows[...], rows_right(dpre), 0, 0)
        dsecond[...] += nt_wide(dpre, wup[: 2 * D, here])
        sums[0:1, here] += row_sum(dpre)
        return carry

    lax.fori_loop(0, PARTS, units, 0)
    dsecond = dsecond[...]
    for image in range(GROUP):
        block_out[image] = result[image * PAD : image * PAD + SEQ] * lives[image]
    dh = dy + normalize_back(dsecond, unit, rate, gain)
    dh_out[...] = dh.reshape(GROUP, PAD, D)
    attended = att[...].reshape(GROUP * PAD, D)
    gout[...] += dot_one(rows_left(dh), rows_right(attended), 0, 0)
    datt_out[...] = dot_one(left_three(dh), wo[...], 1, 0).reshape(GROUP, PAD, D)
    sums[1:2, :D] += row_sum(dsecond * unit)
    sums[2:3, :D] += row_sum(dsecond)
    sums[3:4, :D] += row_sum(dh)
    sums[4:5, :D] += row_sum(dy)

    @pl.when(step == pl.num_programs(0) - 1)
    def _():
        gout_out[...] = gout[...]
        pitch = padded_rows(dp_size)
        if pitch != rows:
            for ref in list(keeps) + list(sends):
                ref[...] = jnp.zeros_like(ref)
        upper = levels(dp_size)[:-1]
        low_count = levels(dp_size)[-1][1]
        for low in range(low_count):

            @pl.when((info[1] & (low_count - 1)) == low)
            def _():
                for j in range(dp_size):
                    at = place_of(info[1] ^ j, upper)
                    here = slice(j * rows, (j + 1) * rows)
                    block = j % low_count
                    there = slice(block * pitch, block * pitch + rows)
                    for slot in range(SLOTS):
                        grad = gup if slot < 2 else gdown
                        base = (slot % 2) * D
                        keeps[low ^ slot][at, there, :] = grad[here, base : base + D]
                        sends[low ^ slot][at, there, :] = grad[here, UNITS + base : UNITS + base + D]


def attention_backward(dp_size, last, groups, first, info, images, qkv, datt, dh, wqkv, vec, *rest):
    if last:
        sums_a, gout, grad_in, keep, send, xs, dqkv, grads, sums, flat = rest
    else:
        grad_in, grads_out, sums_out, xs, dqkv, grads, sums = rest
    step = pl.program_id(0)
    rows = D // dp_size

    @pl.when(step == 0)
    def _():
        xs[...] = jnp.zeros_like(xs)
        grads[...] = jnp.zeros_like(grads)
        sums[...] = jnp.zeros_like(sums)

    xs[:, :SEQ, :] = images[...]
    tokens = xs[...].reshape(GROUP * PAD, D)
    unit, rate = normalize(tokens)
    gain = vec[0:1, :D]
    normed = unit * gain + vec[0:1, 2 * D : 3 * D]
    line = lax.broadcasted_iota(jnp.int32, (PAD, 2 * COLUMNS), 0)

    def head_pair(index, carry):
        image = index // (HEADS // 2)
        pair = index % (HEADS // 2)
        part = pl.ds(pl.multiple_of(image * PAD, 16), PAD)

        def at(base):
            return pl.ds(pl.multiple_of(base + pair * 128, 128), 128)

        query = split(stack_pair(qkv[image, :, at(0)] * 0.125))
        grad_o = split(stack_pair(datt[image, :, at(0)]))
        key_high, key_low = split(qkv[image, :, at(D)])
        value_high, value_low = split(qkv[image, :, at(2 * D)])
        scores = dot_one(
            lanes(key_high, key_high, key_low), lanes(query[0], query[1], query[0]), 1, 1
        )
        scores = jnp.where(line < SEQ, scores, -1e30)
        weights = jnp.exp(scores - jnp.max(scores, axis=0, keepdims=True))
        weights = weights * (1.0 / jnp.sum(weights, axis=0, keepdims=True))
        dweights = dot_one(
            lanes(value_high, value_high, value_low), lanes(grad_o[0], grad_o[1], grad_o[0]), 1, 1
        )
        delta = jnp.sum(weights * dweights, axis=0, keepdims=True)
        weights_high, weights_low = split(weights)
        ds_high, ds_low = split(weights * (dweights - delta))
        dqkv[part, at(2 * D)] = pair_product(weights_high, weights_low, grad_o)
        dqkv[part, at(D)] = pair_product(ds_high, ds_low, query)
        both = dot_one(lanes(key_high, key_low), ds_high, 0, 0)
        turned = both[:128] + (both[128:] + dot_one(key_high, ds_low, 0, 0))
        turned = lines(turned[:HEAD_DIM, :COLUMNS], turned[HEAD_DIM:, COLUMNS:])
        dqkv[part, at(0)] = turned.T[:PAD] * 0.125
        return carry

    lax.fori_loop(0, GROUP * HEADS // 2, head_pair, 0, unroll=UNROLL)
    dall = dqkv[...]
    grads[...] += dot_one(rows_left(normed), rows_right(dall), 0, 0)
    dnormed = nt_wide(dall, wqkv[...])
    dx = dh[...].reshape(GROUP * PAD, D) + normalize_back(dnormed, unit, rate, gain)
    for image in range(GROUP):
        grad_in[image] = dx[image * PAD : image * PAD + SEQ]
    sums[0:1, :] += row_sum(dall)
    sums[1:2, :D] += row_sum(dnormed * unit)
    sums[2:3, :D] += row_sum(dnormed)

    @pl.when(step == pl.num_programs(0) - 1)
    def _():
        if not last:
            grads_out[...] = grads[...]
            sums_out[...] = sums[...]
            return
        is_first = info[0] == 0
        total = sums[0:1, :]
        query_sum = total[:, :D]
        value_sum = total[:, 2 * D :]
        flat[0:1, :D] = sums[1:2, :D]
        flat[0:1, D : 2 * D] = sums_a[1:2, :D]
        flat[0:1, 2 * D : 3 * D] = sums[2:3, :D]
        flat[0:1, 3 * D : 4 * D] = sums_a[2:3, :D]
        flat[0:1, 4 * D : 5 * D] = relative(query_sum, is_first)
        flat[0:1, 5 * D : 6 * D] = relative(value_sum, is_first)
        flat[0:1, 6 * D : 7 * D] = sums_a[3:4, :D]
        flat[0:1, 7 * D : 8 * D] = sums_a[4:5, :D]
        flat[0:1, 8 * D :] = relative(sums_a[0:1, :], is_first)
        pitch = padded_rows(dp_size)
        clear = 0 if pitch != rows else 2 * pitch
        blank = jnp.zeros(keep.shape[:2] + (keep.shape[2] - clear, D), f32)
        keep[:, :, clear:, :] = blank
        send[:, :, clear:, :] = blank
        upper = levels(dp_size)[:-1]
        low_count = levels(dp_size)[-1][1]
        low = info[1] & (low_count - 1)
        piece = VEC // (2 * dp_size)
        for j in range(dp_size):
            at = place_of(info[1] ^ j, upper)
            here = slice(j * rows, (j + 1) * rows)
            block = j % low_count
            one = flat[0:1, 2 * j * piece : (2 * j + 1) * piece]
            two = flat[0:1, (2 * j + 1) * piece : (2 * j + 2) * piece]
            keep[low ^ block, at, 2 * pitch : 2 * pitch + 1, :piece] = jnp.where(is_first, one, two)
            send[low ^ block, at, 2 * pitch : 2 * pitch + 1, :piece] = jnp.where(is_first, two, one)
            for slot in range(SLOTS):
                place = block ^ slot
                there = slice((place % 2) * pitch, (place % 2) * pitch + rows)
                lanes = slice((place // 2) * HALF, (place // 2 + 1) * HALF)
                if slot < 3:
                    mine = grads[here, slot * D : slot * D + HALF]
                    theirs = grads[here, slot * D + HALF : (slot + 1) * D]
                else:
                    mine = gout[here, :HALF]
                    theirs = gout[here, HALF:]
                keep[low ^ slot, at, there, lanes] = mine
                send[low ^ slot, at, there, lanes] = theirs


def params():
    return pltpu.CompilerParams(vmem_limit_bytes=VMEM_BYTES, dimension_semantics=("arbitrary",))


def whole(shape):
    return pl.BlockSpec(shape, lambda g, info: (0,) * len(shape), pipeline_mode=ONCE)


def per_group(shape, first=0):
    return pl.BlockSpec((GROUP,) + shape, lambda g, info: (first + g,) + (0,) * len(shape))


def half_images(groups, first=0):
    return pl.BlockSpec((GROUP, SEQ, D), lambda g, info: (info[0] * groups + first + g, 0, 0))


def shaped(*shape):
    return jax.ShapeDtypeStruct(shape, f32)


def call(kernel, groups, in_specs, out_specs, out_shape, scratch, cost, aliases=None):
    return pl.pallas_call(
        kernel,
        grid_spec=pltpu.PrefetchScalarGridSpec(
            num_scalar_prefetch=1,
            grid=(groups,),
            in_specs=in_specs,
            out_specs=out_specs,
            scratch_shapes=[pltpu.VMEM(s, f32) if isinstance(s, tuple) else s for s in scratch],
        ),
        out_shape=out_shape,
        input_output_aliases=aliases or {},
        compiler_params=params(),
        cost_estimate=pl.CostEstimate(flops=cost, bytes_accessed=20 * 2**20, transcendentals=0),
    )


def polynomial(gram):
    pair = split(gram)
    return ns_second * gram + ns_third * nn(pair, pair)


def eye(size):
    line = lax.broadcasted_iota(jnp.int32, (size, size), 0)
    column = lax.broadcasted_iota(jnp.int32, (size, size), 1)
    return jnp.where(line == column, 1.0, 0.0).astype(f32)


def norm_scale(total):
    return 1.0 / (jnp.sqrt(jnp.full((1, 1), total, f32)) + 1e-07)


def gram_part(block, out):
    pair = split(block[...])
    out[...] = nt(pair, pair)


def product(left, right):
    return dot_one(left_three(left), weights_three(right), 1, 0)


def newton(info, gram_ref, own, other, out):
    half = own.shape[0]
    rows = (out.shape[0]) // 2

    @pl.when(info[0] == 0)
    def _():
        gram = gram_ref[...]
        ident = eye(gram.shape[0])
        scale = norm_scale(jnp.sum(gram * ident))
        gram = gram * (scale * scale)
        total = None
        for sweep in range(NS_STEPS):
            left, right = left_three(gram), weights_three(gram)
            mixing = ns_first * ident + ns_second * gram + ns_third * dot_one(left, right, 1, 0)
            mixing_right = weights_three(mixing)
            total = mixing if total is None else dot_one(left_three(total), mixing_right, 1, 0)
            if sweep < NS_STEPS - 1:
                gram = dot_one(left_three(dot_one(left, mixing_right, 1, 0)), mixing_right, 1, 0)
        factor = jnp.where(info[3] >= 2, -2.0, -1.0).astype(f32) * matrix_rate
        out[...] = total[: out.shape[0]] * (scale * factor)

    @pl.when(info[0] != 0)
    def _():
        matrix = lanes(
            lines(own[:, :HALF], own[:, HALF:]),
            lines(other[:, :HALF], other[:, HALF:]),
        )
        matrix = matrix * norm_scale(jnp.sum(matrix * matrix))
        for sweep in range(NS_STEPS):
            high, low = split(matrix)
            square = dot_one(lanes(high, high, low), lanes(high, low, high), 1, 1)
            mixing = ns_second * square + ns_third * product(square, square)
            matrix = ns_first * matrix + dot_one(left_three(mixing), lines(high, low, high), 1, 0)
        matrix = matrix * (-matrix_rate)
        for column in range(2):
            lane = slice(column * HALF, (column + 1) * HALF)
            there = slice(column * rows, (column + 1) * rows)
            if out.shape[1] > D:
                out[there, D:] = jnp.zeros((rows, out.shape[1] - D), f32)
            out[there, :HALF] = matrix[:rows, lane]
            out[there, HALF:D] = matrix[half : half + rows, lane]


def plain(kernel, operands, out_shape, cost):
    return pl.pallas_call(
        kernel,
        in_specs=[
            pl.BlockSpec(memory_space=pltpu.SMEM if x.ndim == 1 else pltpu.VMEM) for x in operands
        ],
        out_specs=jax.tree.map(lambda _: pl.BlockSpec(memory_space=pltpu.VMEM), out_shape),
        out_shape=out_shape,
        compiler_params=pltpu.CompilerParams(vmem_limit_bytes=VMEM_BYTES // 2),
        cost_estimate=pl.CostEstimate(flops=cost, bytes_accessed=5 * 2**20, transcendentals=0),
    )(*operands)


def pass_on():
    pass


def open_plane(count, keep, got, momenta, total):
    total[:count] = (keep[...] + got[...]).reshape(count, D)
    total[count:] = momenta[...]


def close_plane(slots, above, pitch, info, own, *rest):
    parts = rest[: slots - 1]
    total, held_wide, held_small = rest[-3:]
    count = above * SLOTS * pitch
    low = info[3]
    blocks = [own] + list(parts)
    value = blocks[0][:count]
    for block in blocks[1:]:
        value = value + block[:count]
    total[...] = value.reshape(total.shape)
    for s, block in enumerate(blocks):
        at = pl.multiple_of((low ^ s) * pitch, 8)
        held_wide[pl.ds(at, pitch), :] = block[count : count + pitch]
        there = slice((s % 2) * pitch, (s % 2 + 1) * pitch)
        held_small[there, (s // 2) * HALF : (s // 2 + 1) * HALF] = block[count + pitch :, :HALF]


def open_upper(size, slots, count, total, *rest):
    wide_parts = rest[: count - 1]
    held_wide, own = rest[count - 1 : count + 1]
    small_parts = rest[count + 1 : count + slots]
    grads, message = rest[-2:]
    value = total[0]
    for part in wide_parts:
        value = value + part[...]
    grads[...] = value
    moment = momentum_decay * held_wide[...] + value
    wide = value.shape[0]
    small = own[0]
    for part in small_parts:
        small = small + part[...]
    small = small.reshape(size, -1, D)
    for s in range(size):
        message[s, :wide] = moment
        message[s, wide:] = small[s]


def close_upper(size, wide, own, *rest):
    parts = rest[: size - 1]
    held_small = rest[size - 1]
    moments, small, moment = rest[-3:]
    value = own[0, wide:]
    moments[:wide] = own[0, :wide]
    for s, part in enumerate(parts):
        moments[(s + 1) * wide : (s + 2) * wide] = part[:wide]
        value = value + part[wide:]
    small[...] = value
    rows = moment.shape[0]
    moment[...] = momentum_decay * held_small[...] + value[:rows]


def join_small(gram, gram_far, own, *rest):
    parts, (gram_sum, joined) = rest[:-2], rest[-2:]
    gram_sum[...] = gram[...] + gram_far[...]
    rows = own.shape[0]
    joined[:rows] = own[...]
    for s, part in enumerate(parts):
        joined[(s + 1) * rows : (s + 2) * rows] = part[...]


def return_messages(rows, pitch, info, result, result_far, block, grads_a, grads_b, message, steps_a):
    low = info[3]
    is_first = info[0] == 0
    steps_a[...] = product(jnp.where(is_first, result[...], result_far[...]), block[...])
    steps_b = jnp.where(is_first, result_far[2 * pitch :, :D], result[: 2 * pitch, :D])
    for s in range(SLOTS):
        at = pl.multiple_of((low ^ s) * pitch, 8)
        message[s, :, :D] = grads_a[pl.ds(at, pitch), :]
        message[s, :, D : 2 * D] = steps_a[pl.ds(at, pitch), :]
        here = slice((s % 2) * pitch, (s % 2 + 1) * pitch)
        lane = slice((s // 2) * HALF, (s // 2 + 1) * HALF)
        message[s, :, 2 * D : 2 * D + HALF] = grads_b[here, lane]
        message[s, :, 2 * D + HALF :] = steps_b[here, lane]


def finish(rows, info, own, *rest):
    parts, momenta, stack = rest[: SLOTS - 1], rest[SLOTS - 1 : SLOTS + 5], rest[-1]
    outs = rest[SLOTS + 5 : -1]
    low = info[3]
    stack[0] = own[0]
    for s, part in enumerate(parts):
        stack[s + 1] = part[...]
    for slot in range(SLOTS):
        block = stack[low ^ slot]
        grad, step, moment = outs[slot], outs[12 + slot], outs[6 + slot]
        value = block[:rows, 2 * D : 2 * D + HALF]
        grad[...] = value
        moment[...] = momentum_decay * momenta[slot][...] + value
        step[...] = block[:rows, 2 * D + HALF :]
        wide = 4 + slot // 2
        here = slice((slot % 2) * D, (slot % 2 + 1) * D)
        value = block[:rows, :D]
        outs[wide][:, here] = value
        outs[6 + wide][:, here] = momentum_decay * momenta[wide][:, here] + value
        outs[12 + wide][:, here] = block[:rows, D : 2 * D]


def gated(kernel, operands, out_shape, passes, scratch=(), cost=10**6, vmem=VMEM_BYTES // 2, after=()):
    def run(*refs):
        count = len(operands) + len(passes) + len(after)
        outs = refs[count : count + len(out_shape)]
        kernel(*refs[: len(operands)], *outs, *refs[count + len(out_shape) + len(passes) :])

    in_specs = []
    arrays = []
    for x in operands:
        if isinstance(x, tuple):
            x, index = x
            block = (1,) + x.shape[1:]
            in_specs.append(pl.BlockSpec(block, lambda g, n=x.ndim, i=index: (i,) + (0,) * (n - 1)))
        elif x.dtype == jnp.int32:
            in_specs.append(pl.BlockSpec(memory_space=pltpu.SMEM))
        else:
            in_specs.append(pl.BlockSpec(x.shape, lambda g, n=x.ndim: (0,) * n))
        arrays.append(x)
    anywhere = pl.BlockSpec(memory_space=pl.ANY)
    result = pl.pallas_call(
        run,
        grid=(1,),
        in_specs=in_specs + [anywhere] * (len(passes) + len(after)),
        out_specs=[pl.BlockSpec(x.shape, lambda g, n=len(x.shape): (0,) * n) for x in out_shape]
        + [anywhere] * len(passes),
        out_shape=list(out_shape) + [shaped(*x.shape) for x in passes],
        scratch_shapes=list(scratch),
        input_output_aliases={
            len(operands) + i: len(out_shape) + i for i in range(len(passes))
        },
        compiler_params=pltpu.CompilerParams(vmem_limit_bytes=vmem),
        cost_estimate=pl.CostEstimate(flops=cost, bytes_accessed=2**20, transcendentals=0),
    )(*arrays, *passes, *after)
    return result


def pick(stack, index):
    return lax.dynamic_index_in_dim(stack, index, 0, keepdims=False)


def body(
    images,
    image_count,
    cotangent,
    w_query,
    w_key,
    w_value,
    w_out,
    w_up,
    w_down,
    vectors,
    mom_query,
    mom_key,
    mom_value,
    mom_out,
    mom_up,
    mom_down,
    adam_first,
    adam_second,
):
    tp_index = lax.axis_index("tp")
    dp_index = lax.axis_index("dp")
    dp_size = lax.axis_size("dp")
    rows = D // dp_size
    pitch = padded_rows(dp_size)
    piece = vectors.shape[0]
    groups = images.shape[0] // (2 * GROUP)
    slots = groups * GROUP
    is_first = tp_index == 0
    every = levels(dp_size)
    upper, plane = every[:-1], every[-1]
    above = dp_size // plane[1]
    low = dp_index & (plane[1] - 1)
    info = jnp.stack([tp_index, dp_index, image_count[0], low]).astype(jnp.int32)

    vec_tail = jnp.pad(vectors, (0, rows * 128 - piece)).reshape(rows, 128)
    shard_one = jnp.concatenate([w_query, w_key, w_value, w_out.T, vec_tail], axis=1)
    shard_two = jnp.concatenate([w_up, w_down.T], axis=1)
    mom_wide = jnp.concatenate([mom_up, mom_down.T], axis=1)
    mom_small = jnp.concatenate([mom_query, mom_key, mom_value, mom_out.T], axis=1)
    ahead = jnp.pad(mom_wide.reshape(rows, SLOTS, D), ((0, pitch - rows), (0, 0), (0, 0)))
    behind = jnp.pad(mom_small.reshape(rows, SLOTS, HALF), ((0, pitch - rows), (0, 0), (0, D - HALF)))
    mom_slots = jnp.concatenate([ahead, behind], axis=0).transpose(1, 0, 2)
    mom_slots = [pick(mom_slots, low ^ s) for s in range(SLOTS)]

    part_one = gather(shard_one[None], upper, dp_size)
    part_one, mom_slots = tie(part_one, mom_slots)
    got_one = exchange(part_one, plane, dp_size)
    upper_parts = [shard_two[None]]
    for level in upper[:-1]:
        upper_parts = [jnp.concatenate(upper_parts + exchange(upper_parts[0], level, dp_size), axis=0)]
    upper_parts = upper_parts + exchange(upper_parts[0], upper[-1], dp_size)
    got_one, upper_parts = tie(got_one, upper_parts)
    part_two = jnp.concatenate(upper_parts, axis=0)
    own_one = [part_one] + got_one
    other_one = [swap_tp(part) for part in own_one]
    got_two = exchange(part_two, plane, dp_size)
    near_two = swap_tp(part_two)

    qkv, att, hid, wqkv, wo, vec = call(
        functools.partial(attention_forward, dp_size),
        groups,
        [
            half_images(groups),
        ]
        + [whole((above, rows, 4 * HALF + 128))] * (2 * SLOTS),
        [
            per_group((PAD, 3 * D)),
            per_group((PAD, D)),
            per_group((PAD, D)),
            whole((3 * D, 3 * D)),
            whole((3 * D, D)),
            whole((1, VEC)),
        ],
        [
            shaped(slots, PAD, 3 * D),
            shaped(slots, PAD, D),
            shaped(slots, PAD, D),
            jax.ShapeDtypeStruct((3 * D, 3 * D), bf16),
            jax.ShapeDtypeStruct((3 * D, D), bf16),
            shaped(1, VEC),
        ],
        [
            (GROUP, PAD, D),
            (D, 4 * D),
            pltpu.VMEM((3 * D, 3 * D), bf16),
            pltpu.VMEM((3 * D, D), bf16),
            (GROUP * PAD, D),
            (1, VEC),
        ],
        16 * 10**9,
    )(info, images, *own_one, *other_one)

    got_two, hid = tie(got_two, hid)
    own_two = [part_two] + got_two
    other_two = [near_two] + [swap_tp(part) for part in got_two]

    block_own, dh, datt, *slots_a = call(
        functools.partial(mlp, dp_size),
        groups,
        [
            per_group((PAD, D)),
            per_group((PAD, D)),
            half_images(groups),
        ]
        + [whole((above, rows, 2 * UNITS))] * (2 * SLOTS)
        + [
            whole((3 * D, D)),
            whole((1, VEC)),
        ],
        [
            per_group((SEQ, D)),
            per_group((PAD, D)),
            per_group((PAD, D)),
        ]
        + [whole((above, SLOTS * pitch, D))] * (2 * SLOTS)
        + [whole((D, D)), whole((8, FF))],
        [
            shaped(slots, SEQ, D),
            shaped(slots, PAD, D),
            shaped(slots, PAD, D),
        ]
        + [shaped(above, SLOTS * pitch, D)] * (2 * SLOTS)
        + [shaped(D, D), shaped(8, FF)],
        [
            pltpu.VMEM((3 * D, FF), bf16),
            pltpu.VMEM((3 * D, FF), bf16),
            (GROUP, PAD, D),
            (D, FF),
            (D, FF),
            (D, D),
            pltpu.VMEM((GROUP * PAD, 3 * D), bf16),
            pltpu.VMEM((GROUP * PAD, 3 * D), bf16),
            pltpu.VMEM((3 * GROUP * PAD, D), bf16),
            pltpu.VMEM((3 * GROUP * PAD, D), bf16),
            (GROUP * PAD, D),
            (GROUP * PAD, D),
            (1, FF),
        ],
        48 * 10**9,
    )(info, hid, att, cotangent, *own_two, *other_two, wo, vec)

    keep_a, send_a, (gout, sums_a) = slots_a[:SLOTS], slots_a[SLOTS : 2 * SLOTS], slots_a[2 * SLOTS :]
    body_rows = above * SLOTS * pitch
    got_a = [swap_tp(send_a[s]) for s in range(SLOTS)]
    sum_a = [
        gated(
            functools.partial(open_plane, body_rows),
            [keep_a[s], got_a[s], mom_slots[s]],
            [shaped(body_rows + 2 * pitch, D)],
            [],
        )[0]
        for s in range(SLOTS)
    ]
    plane_a = [swap_dp(sum_a[s], s, dp_size) for s in range(1, plane[1])]
    (sums_a,) = gated(pass_on, [], [], [sums_a], after=sum_a)

    def backward(last, first, count, operands, extra_in, before, extra_out_specs, extra_out, extra_scratch):
        return call(
            functools.partial(attention_backward, dp_size, last, groups, first),
            count,
            [
                half_images(groups, first),
                per_group((PAD, 3 * D), first),
                per_group((PAD, D), first),
                per_group((PAD, D), first),
                whole((2 * D, 3 * D)),
                whole((1, VEC)),
            ]
            + [whole(x.shape) for x in extra_in]
            + [pl.BlockSpec(memory_space=pl.ANY)] * len(before),
            [per_group((SEQ, D), first)] + extra_out_specs,
            [shaped(slots, SEQ, D)] + extra_out,
            [(GROUP, PAD, D), (GROUP * PAD, 3 * D), (D, 3 * D), (8, 3 * D)] + extra_scratch,
            10 * 10**9 * count,
            {len(operands) + len(extra_in): 0} if before else {},
        )(*operands, *extra_in, *before)

    small = (SLOTS, above, 2 * pitch + 8, D)
    grad_own, keep_b, send_b = backward(
        True,
        0,
        groups,
        (info, images, qkv, datt, dh, wqkv, vec),
        [sums_a, gout],
        [],
        [whole(small), whole(small)],
        [shaped(*small), shaped(*small)],
        [(1, VEC)],
    )
    total_a, held_wide, held_small, send_b = gated(
        functools.partial(close_plane, SLOTS, above, pitch),
        [info, sum_a[0]] + plane_a,
        [shaped(above, SLOTS * pitch, D), shaped(SLOTS * pitch, D), shaped(2 * pitch, D)],
        [send_b],
    )
    sum_b = (keep_b + swap_tp(send_b)).reshape((SLOTS, above) + small[2:])
    plane_b = [swap_dp(sum_b[s], s, dp_size) for s in range(1, plane[1])]
    total_a = scatter_sum(total_a, upper[1:], dp_size)
    shift, size = upper[0]
    total_a = total_a.reshape(size, SLOTS * pitch, D)
    upper_a = [swap_dp(total_a[s], s << shift, dp_size) for s in range(1, size)]

    def both_halves(mine):
        theirs = swap_tp(mine)
        return jnp.concatenate(
            [jnp.where(is_first, mine, theirs), jnp.where(is_first, theirs, mine)], axis=0
        )

    first_shift, first_size = upper[-1]
    count = above // first_size * (2 * pitch + 8)
    grads_a, message, block_own, grad_own = gated(
        functools.partial(open_upper, first_size, SLOTS, size),
        [(total_a, 0)] + upper_a + [held_wide, (sum_b, 0)] + plane_b,
        [shaped(SLOTS * pitch, D), shaped(first_size, SLOTS * pitch + count, D)],
        [block_own, grad_own],
    )
    block_out = both_halves(block_own)
    input_grad = both_halves(grad_own)
    got = [swap_dp(message[s], s << first_shift, dp_size) for s in range(1, first_size)]
    all_a, total_b, new_b, block_out, input_grad = gated(
        functools.partial(close_upper, first_size, SLOTS * pitch),
        [(message, 0)] + got + [held_small],
        [shaped(first_size * SLOTS * pitch, D), shaped(count, D), shaped(2 * pitch, D)],
        [block_out, input_grad],
    )
    if len(upper) > 1:
        all_a = gather(all_a[None], upper[:-1][::-1], dp_size).reshape(-1, D)
        total_b = scatter_sum(total_b.reshape(-1, 2 * pitch + 8, D), upper[:-1], dp_size)[0]
        new_b = momentum_decay * held_small + total_b[: 2 * pitch]
    grad_vectors = total_b[2 * pitch, :piece]
    grads_b = total_b[: 2 * pitch]

    part_b = gather(new_b[None], upper[:-1], dp_size).reshape(-1, D)
    parts_b = exchange(part_b, upper[-1], dp_size)
    size = all_a.shape[0]
    gram = plain(gram_part, (all_a,), shaped(size, size), 10**9)
    gram = gram + swap_tp(gram)
    gram_half = lax.dynamic_slice_in_dim(gram, tp_index * (size // 2), size // 2, 0)
    gram_half, all_b = gated(
        join_small,
        [gram_half, swap_dp(gram_half, 1, dp_size), part_b] + parts_b,
        [shaped(size // 2, size), shaped(part_b.shape[0] * (len(parts_b) + 1), D)],
        [],
    )
    gram_other = swap_tp(gram_half)
    gram = jnp.concatenate(
        [jnp.where(is_first, gram_half, gram_other), jnp.where(is_first, gram_other, gram_half)]
    )
    (result,) = gated(
        newton,
        [info, gram, all_b, swap_tp(all_b)],
        [shaped(SLOTS * pitch, size)],
        [],
        cost=12 * 10**9,
    )
    result_far = swap_tp(result)

    (message,) = gated(
        functools.partial(return_messages, rows, pitch),
        [info, result, result_far, all_a, grads_a, grads_b],
        [shaped(SLOTS, pitch, 3 * D)],
        [],
        [pltpu.VMEM((SLOTS * pitch, D), f32)],
    )
    got = [swap_dp(message[s], s, dp_size) for s in range(1, plane[1])]
    momenta = [mom_query, mom_key, mom_value, mom_out.T, mom_up, mom_down.T]
    kinds = [shaped(rows, HALF)] * 4 + [shaped(rows, UNITS)] * 2
    results = gated(
        functools.partial(finish, rows),
        [info, (message, 0)] + got + momenta,
        kinds * 3,
        [],
        [pltpu.VMEM((SLOTS, pitch, 3 * D), f32)],
    )

    def in_order(six):
        return (six[0], six[1], six[2], six[3].T, six[4], six[5].T)

    weight_grads = in_order(results[:6])
    new_momenta = in_order(results[6:12])
    steps = in_order(results[12:])

    first_new = adam_beta_one * adam_first + (1.0 - adam_beta_one) * grad_vectors
    second_new = adam_beta_two * adam_second + (1.0 - adam_beta_two) * grad_vectors * grad_vectors
    first_hat = first_new / (1.0 - adam_beta_one**STEP)
    second_hat = second_new / (1.0 - adam_beta_two**STEP)
    vector_update = -adam_rate * (
        first_hat / (jnp.sqrt(second_hat) + adam_eps) + adam_decay * vectors
    )
    return (
        (block_out, input_grad)
        + weight_grads
        + (grad_vectors,)
        + new_momenta
        + steps
        + (first_new, second_new, vector_update)
    )


def solution(mesh):
    image = P("dp", None, None)
    wide = P("dp", "tp")
    tall = P("tp", "dp")
    flat = P(("dp", "tp"))
    six = (wide, wide, wide, tall, wide, tall)
    in_specs = (image, P("dp"), image) + six + (flat,) + six + (flat, flat)
    out_specs = (image, image) + six + (flat,) + six + six + (flat, flat, flat)
    return jax.shard_map(body, mesh=mesh, in_specs=in_specs, out_specs=out_specs, check_vma=False)
```

profile of v0, /device:TPU:0, one launch (start us, length us, event | category | flops | bytes accessed | tf_op | source)
XLA Modules:
  0.0 258.1 jit_solution(9127761447732281825)
XLA Ops:
  2.3 3.1 %collective-permute-start = (f32[1,24,896]{2,1,0:T(8,128)S(1)}, f32[1,24,896]{2,1,0:T(8,128)S(1)}, u32[]{:S(2)}, u32[]{:S(2)}) collective-permute-start(f32[1,24,896]{2,1,0:T(8,128)S(1)} %bitcast.55), channel_id=1, source_target_pairs={{0,8},{2,10},{4,12},{6,14},{8,0},{10,2},{12,4},{14,6},{16,24},{18,... | collective-permute-start | bytes 258056 | tf_op jit(solution)/shard_map/ppermute | solution.py:95
  5.4 2.6 %collective-permute-start.1 = (f32[1,24,896]{2,1,0:T(8,128)S(1)}, f32[1,24,896]{2,1,0:T(8,128)S(1)}, u32[]{:S(2)}, u32[]{:S(2)}) collective-permute-start(f32[1,24,896]{2,1,0:T(8,128)S(1)} %bitcast.56), channel_id=1, source_target_pairs={{0,16},{2,18},{4,20},{6,22},{8,24},{10,26},{12,28},{14,30},{16,0},... | collective-permute-start | bytes 258056 | tf_op jit(solution)/shard_map/ppermute | solution.py:95
  10.4 4.5 %collective-permute-done.1 = f32[1,24,896]{2,1,0:T(8,128)S(1)} collective-permute-done((f32[1,24,896]{2,1,0:T(8,128)S(1)}, f32[1,24,896]{2,1,0:T(8,128)S(1)}, u32[]{:S(2)}, u32[]{:S(2)}) %collective-permute-start.1) | collective-permute-done | bytes 86048 | tf_op jit(solution)/shard_map/ppermute | solution.py:95
  14.9 1.6 collective-permute-start.3
  20.0 1.6 collective-permute-start.7
  21.6 2.6 collective-permute-done.6
  24.1 3.2 %collective-permute-start.8 = (f32[1,24,1536]{2,1,0:T(8,128)S(1)}, f32[1,24,1536]{2,1,0:T(8,128)S(1)}, u32[]{:S(2)}, u32[]{:S(2)}) collective-permute-start(f32[1,24,1536]{2,1,0:T(8,128)S(1)} %maximum_bitcast_fusion), channel_id=1, source_target_pairs={{0,24},{2,26},{4,28},{6,30},{8,16},{10,18},{12,20},{14,22},{16,8},... | collective-permute-start | bytes 442376 | tf_op jit(solution)/shard_map/ppermute | solution.py:95
  28.6 3.7 %collective-permute-done.7 = f32[1,24,1536]{2,1,0:T(8,128)S(1)} collective-permute-done((f32[1,24,1536]{2,1,0:T(8,128)S(1)}, f32[1,24,1536]{2,1,0:T(8,128)S(1)}, u32[]{:S(2)}, u32[]{:S(2)}) %collective-permute-start.7) | collective-permute-done | bytes 147488 | tf_op jit(solution)/shard_map/ppermute | solution.py:95
  33.5 1.6 collective-permute-start.10
  38.0 23.2 %shard_map.361 = (f32[6,208,1152]{2,1,0:T(8,128)}, f32[6,208,384]{2,1,0:T(8,128)}, f32[6,208,384]{2,1,0:T(8,128)}, bf16[1152,1152]{1,0:T(8,128)(2,1)}, bf16[1152,384]{1,0:T(8,128)(2,1)}, /*index=5*/f32[1,4608]{1,0:T(1,128)}) custom-call(s32[4]{0:T(128)} %pad_add_fusion.info.refs_0_, f32[12,197,384]{2,1,0:T(8,128)} %images.3, f32[4,24,896]{2,1,0:T(8,128)} %copy-done.16, ...), custom_call_target="tpu_custom_call" | custom-call | flops 16000000000 | bytes 20971520 | tf_op jit(solution)/shard_map/pallas_call | solution.py:852
  61.5 1.6 collective-permute-done.9.rest_1_
  63.6 2.5 collective-permute-done.17.rest_5_
  67.8 47.6 %shard_map.362 = (f32[6,197,384]{2,1,0:T(8,128)}, f32[6,208,384]{2,1,0:T(8,128)}, f32[6,208,384]{2,1,0:T(8,128)}, f32[4,96,384]{2,1,0:T(8,128)}, f32[4,96,384]{2...) custom-call(s32[4]{0:T(128)} %pad_add_fusion.info.refs_0_, ...), custom_call_target="tpu_custom_call" | custom-call | flops 48000000000 | bytes 20971520 | tf_op jit(solution)/shard_map/pallas_call | solution.py:890
  118.9 2.3 collective-permute-start.26
  123.5 43.9 %shard_map.368 = (f32[6,197,384]{2,1,0:T(8,128)}, f32[4,4,56,384]{3,2,1,0:T(8,128)}, f32[4,4,56,384]{3,2,1,0:T(8,128)}) custom-call(s32[4]{0:T(128)} %pad_add_fusion.info.refs_0_, f32[12,197,384]{2,1,0:T(8,128)} %images.3, f32[6,208,1152]{2,1,0:T(8,128)} %get-tuple-element.123.qkv, f32[6,208,384]{2,1,0:T(8,128)} %get-tuple-element.124.datt, ...), custom_call_target="tpu_custom_call" | custom-call | flops 30000001024 | bytes 20971520 | tf_op jit(solution)/shard_map/pallas_call | solution.py:951
  170.3 3.1 %collective-permute-done.30 = f32[4,4,56,384]{3,2,1,0:T(8,128)S(1)} collective-permute-done((f32[4,4,56,384]{3,2,1,0:T(8,128)S(1)}, f32[4,4,56,384]{3,2,1,0:T(8,128)S(1)}, u32[]{:S(2)}, u32[]{:S(2)}) %collective-permute-start.30) | collective-permute-done | bytes 1376288 | tf_op jit(solution)/shard_map/ppermute | solution.py:99
  177.2 1.9 collective-permute-start.27
  180.2 4.1 %collective-permute-done.27.refs_1_ = f32[96,384]{1,0:T(8,128)S(1)} collective-permute-done((f32[96,384]{1,0:T(8,128)S(1)}, f32[96,384]{1,0:T(8,128)S(1)}, u32[]{:S(2)}, u32[]{:S(2)}) %collective-permute-start.27) | collective-permute-done | bytes 147488 | tf_op jit(solution)/shard_map/ppermute | solution.py:95
  184.2 1.6 collective-permute-start.29
  185.8 6.4 %collective-permute-done.28.refs_2_ = f32[96,384]{1,0:T(8,128)S(1)} collective-permute-done((f32[96,384]{1,0:T(8,128)S(1)}, f32[96,384]{1,0:T(8,128)S(1)}, u32[]{:S(2)}, u32[]{:S(2)}) %collective-permute-start.28) | collective-permute-done | bytes 147488 | tf_op jit(solution)/shard_map/ppermute | solution.py:95
  193.0 2.7 %collective-permute-start.34 = (f32[152,384]{1,0:T(8,128)S(1)}, f32[152,384]{1,0:T(8,128)S(1)}, u32[]{:S(2)}, u32[]{:S(2)}) collective-permute-start(f32[152,384]{1,0:T(8,128)S(1)} %get-tuple-element.178), channel_id=1, source_target_pairs={{0,8},{2,10},{4,12},{6,14},{8,0},{10,2},{12,4},{14,6},{16,24},{18,... | collective-permute-start | bytes 700424 | tf_op jit(solution)/shard_map/ppermute | solution.py:95
  198.4 2.3 broadcast_select_fusion.1
  200.7 1.7 broadcast_select_fusion.3
  202.5 2.1 pad_maximum_fusion.1.refs_6_
  204.6 2.1 pad_maximum_fusion.refs_5_
  206.7 8.5 %collective-permute-done.35.refs_2_ = f32[152,384]{1,0:T(8,128)S(1)} collective-permute-done((f32[152,384]{1,0:T(8,128)S(1)}, f32[152,384]{1,0:T(8,128)S(1)}, u32[]{:S(2)}, u32[]{:S(2)}) %collective-permute-start.35) | collective-permute-done | bytes 233504 | tf_op jit(solution)/shard_map/ppermute | solution.py:95
  216.1 2.0 collective-permute-done.39
  219.6 4.4 %collective-permute-start.41 = (f32[48,384]{1,0:T(8,128)S(1)}, f32[48,384]{1,0:T(8,128)S(1)}, u32[]{:S(2)}, u32[]{:S(2)}) collective-permute-start(f32[48,384]{1,0:T(8,128)S(1)} %get-tuple-element.143.refs_2_), channel_id=1, source_target_pairs={{0,8},{2,10},{4,12},{6,14},{8,0},{10,2},{12,4},{14,6},{16,24},{18,... | collective-permute-start | bytes 221192 | tf_op jit(solution)/shard_map/ppermute | solution.py:95
  226.7 5.9 %collective-permute-done.42.refs_4_ = f32[48,384]{1,0:T(8,128)S(1)} collective-permute-done((f32[48,384]{1,0:T(8,128)S(1)}, f32[48,384]{1,0:T(8,128)S(1)}, u32[]{:S(2)}, u32[]{:S(2)}) %collective-permute-start.42) | collective-permute-done | bytes 73760 | tf_op jit(solution)/shard_map/ppermute | solution.py:95
  234.7 10.6 %shard_map.374.refs_1_ = f32[96,384]{1,0:T(8,128)S(1)} custom-call(s32[4]{0:T(128)S(1)} %copy-done.14, f32[384,384]{1,0:T(8,128)S(1)} %pad_maximum_fusion.2.refs_1_, f32[192,384]{1,0:T(8,128)S(1)} %get-tuple-element.145.refs_2_, f32[192,384]{1,0:T(8,128)S(1)} %collective-permute-done.45.refs_3_), custom_call_target="tpu_custom_call" | custom-call | flops 12000000000 | bytes 1048576 | tf_op jit(solution)/shard_map/pallas_call | solution.py:772
  248.5 1.6 collective-permute-start.48
  252.0 1.8 collective-permute-done.47.refs_2_
  (180 shorter events, 47.7 us)
Async XLA Ops:
  2.3 8.1 %collective-permute-start = (f32[1,24,896]{2,1,0:T(8,128)S(1)}, f32[1,24,896]{2,1,0:T(8,128)S(1)}, u32[]{:S(2)}, u32[]{:S(2)}) collective-permute-start(f32[1,24,896]{2,1,0:T(8,128)S(1)} %bitcast.55), channel_id=1, source_target_pairs={{0,8},{2,10},{4,12},{6,14},{8,0},{10,2},{12,4},{14,6},{16,24},{18,... | collective-permute-start | bytes 258056 | tf_op jit(solution)/shard_map/ppermute | solution.py:95
  5.4 9.5 %collective-permute-start.1 = (f32[1,24,896]{2,1,0:T(8,128)S(1)}, f32[1,24,896]{2,1,0:T(8,128)S(1)}, u32[]{:S(2)}, u32[]{:S(2)}) collective-permute-start(f32[1,24,896]{2,1,0:T(8,128)S(1)} %bitcast.56), channel_id=1, source_target_pairs={{0,16},{2,18},{4,20},{6,22},{8,24},{10,26},{12,28},{14,30},{16,0},... | collective-permute-start | bytes 258056 | tf_op jit(solution)/shard_map/ppermute | solution.py:95
  8.0 6.9 %collective-permute-start.2 = (f32[1,24,896]{2,1,0:T(8,128)S(1)}, f32[1,24,896]{2,1,0:T(8,128)S(1)}, u32[]{:S(2)}, u32[]{:S(2)}) collective-permute-start(f32[1,24,896]{2,1,0:T(8,128)S(1)} %bitcast.57), channel_id=1, source_target_pairs={{0,24},{2,26},{4,28},{6,30},{8,16},{10,18},{12,20},{14,22},{16,8},... | collective-permute-start | bytes 258056 | tf_op jit(solution)/shard_map/ppermute | solution.py:95
  14.9 17.4 %collective-permute-start.3 = (f32[4,24,896]{2,1,0:T(8,128)S(1)}, f32[4,24,896]{2,1,0:T(8,128)}, u32[]{:S(2)}, u32[]{:S(2)}) collective-permute-start(f32[4,24,896]{2,1,0:T(8,128)S(1)} %pad_maximum_fusion.3.rest_0_), channel_id=1, source_target_pairs={{0,2},{2,0},{4,6},{6,4},{8,10},{10,8},{12,14},{14,12},{16,18},{18,... | collective-permute-start | bytes 1032200 | tf_op jit(solution)/shard_map/ppermute | solution.py:95
  16.5 15.9 %collective-permute-start.4 = (f32[4,24,896]{2,1,0:T(8,128)S(1)}, f32[4,24,896]{2,1,0:T(8,128)}, u32[]{:S(2)}, u32[]{:S(2)}) collective-permute-start(f32[4,24,896]{2,1,0:T(8,128)S(1)} %pad_maximum_fusion.3.rest_0_), channel_id=1, source_target_pairs={{0,4},{2,6},{4,0},{6,2},{8,12},{10,14},{12,8},{14,10},{16,20},{18,... | collective-permute-start | bytes 1032200 | tf_op jit(solution)/shard_map/ppermute | solution.py:95
  18.0 14.3 %collective-permute-start.5 = (f32[4,24,896]{2,1,0:T(8,128)S(1)}, f32[4,24,896]{2,1,0:T(8,128)}, u32[]{:S(2)}, u32[]{:S(2)}) collective-permute-start(f32[4,24,896]{2,1,0:T(8,128)S(1)} %pad_maximum_fusion.3.rest_0_), channel_id=1, source_target_pairs={{0,6},{2,4},{4,2},{6,0},{8,14},{10,12},{12,10},{14,8},{16,22},{18,... | collective-permute-start | bytes 1032200 | tf_op jit(solution)/shard_map/ppermute | solution.py:95
  20.0 12.3 %collective-permute-start.7 = (f32[1,24,1536]{2,1,0:T(8,128)S(1)}, f32[1,24,1536]{2,1,0:T(8,128)S(1)}, u32[]{:S(2)}, u32[]{:S(2)}) collective-permute-start(f32[1,24,1536]{2,1,0:T(8,128)S(1)} %maximum_bitcast_fusion), channel_id=1, source_target_pairs={{0,16},{2,18},{4,20},{6,22},{8,24},{10,26},{12,28},{14,30},{16,0},... | collective-permute-start | bytes 442376 | tf_op jit(solution)/shard_map/ppermute | solution.py:95
  24.1 8.2 %collective-permute-start.8 = (f32[1,24,1536]{2,1,0:T(8,128)S(1)}, f32[1,24,1536]{2,1,0:T(8,128)S(1)}, u32[]{:S(2)}, u32[]{:S(2)}) collective-permute-start(f32[1,24,1536]{2,1,0:T(8,128)S(1)} %maximum_bitcast_fusion), channel_id=1, source_target_pairs={{0,24},{2,26},{4,28},{6,30},{8,16},{10,18},{12,20},{14,22},{16,8},... | collective-permute-start | bytes 442376 | tf_op jit(solution)/shard_map/ppermute | solution.py:95
  33.5 28.0 %collective-permute-start.10 = (f32[4,24,1536]{2,1,0:T(8,128)S(1)}, f32[4,24,1536]{2,1,0:T(8,128)S(1)}, u32[]{:S(2)}, u32[]{:S(2)}) collective-permute-start(f32[4,24,1536]{2,1,0:T(8,128)S(1)} %constant_dynamic-update-slice_fusion.rest_0_), channel_id=1, source_target_pairs={{0,4},{2,6},{4,0},{6,2},{8,12},{10,14},{12,8},{14,10},{16,20},{18,... | collective-permute-start | bytes 1769480 | tf_op jit(solution)/shard_map/ppermute | solution.py:95
  35.1 26.4 %collective-permute-start.11 = (f32[4,24,1536]{2,1,0:T(8,128)S(1)}, f32[4,24,1536]{2,1,0:T(8,128)S(1)}, u32[]{:S(2)}, u32[]{:S(2)}) collective-permute-start(f32[4,24,1536]{2,1,0:T(8,128)S(1)} %constant_dynamic-update-slice_fusion.rest_0_), channel_id=1, source_target_pairs={{0,6},{2,4},{4,2},{6,0},{8,14},{10,12},{12,10},{14,8},{16,22},{18,... | collective-permute-start | bytes 1769480 | tf_op jit(solution)/shard_map/ppermute | solution.py:95
  36.5 26.5 %collective-permute-start.9 = (f32[4,24,1536]{2,1,0:T(8,128)S(1)}, f32[4,24,1536]{2,1,0:T(8,128)}, u32[]{:S(2)}, u32[]{:S(2)}) collective-permute-start(f32[4,24,1536]{2,1,0:T(8,128)S(1)} %constant_dynamic-update-slice_fusion.rest_0_), channel_id=1, source_target_pairs={{0,2},{2,0},{4,6},{6,4},{8,10},{10,8},{12,14},{14,12},{16,18},{18,... | collective-permute-start | bytes 1769480 | tf_op jit(solution)/shard_map/ppermute | solution.py:95
  38.0 25.6 %collective-permute-start.16 = (f32[4,24,1536]{2,1,0:T(8,128)S(1)}, f32[4,24,1536]{2,1,0:T(8,128)}, u32[]{:S(2)}, u32[]{:S(2)}) collective-permute-start(f32[4,24,1536]{2,1,0:T(8,128)S(1)} %constant_dynamic-update-slice_fusion.rest_0_), channel_id=1, source_target_pairs={{0,1},{1,0},{2,3},{3,2},{4,5},{5,4},{6,7},{7,6},{8,9},{9,8},{10,11... | collective-permute-start | bytes 1769480 | tf_op jit(solution)/shard_map/ppermute | solution.py:99
  116.2 6.5 %collective-permute-start.20 = (f32[4,96,384]{2,1,0:T(8,128)}, f32[4,96,384]{2,1,0:T(8,128)S(1)}, u32[]{:S(2)}, u32[]{:S(2)}) collective-permute-start(f32[4,96,384]{2,1,0:T(8,128)} %get-tuple-element.112), channel_id=1, source_target_pairs={{0,1},{1,0},{2,3},{3,2},{4,5},{5,4},{6,7},{7,6},{8,9},{9,8},{10,11... | collective-permute-start | bytes 1769480 | tf_op jit(solution)/shard_map/ppermute | solution.py:99
  118.9 48.5 %collective-permute-start.26 = (f32[432,384]{1,0:T(8,128)S(1)}, f32[432,384]{1,0:T(8,128)S(1)}, u32[]{:S(2)}, u32[]{:S(2)}) collective-permute-start(f32[432,384]{1,0:T(8,128)S(1)} %shard_map.366.refs_4_), channel_id=1, source_target_pairs={{0,6},{2,4},{4,2},{6,0},{8,14},{10,12},{12,10},{14,8},{16,22},{18,... | collective-permute-start | bytes 1990664 | tf_op jit(solution)/shard_map/ppermute | solution.py:95
  121.2 46.2 %collective-permute-start.24 = (f32[432,384]{1,0:T(8,128)S(1)}, f32[432,384]{1,0:T(8,128)S(1)}, u32[]{:S(2)}, u32[]{:S(2)}) collective-permute-start(f32[432,384]{1,0:T(8,128)S(1)} %shard_map.365.refs_3_), channel_id=1, source_target_pairs={{0,4},{2,6},{4,0},{6,2},{8,12},{10,14},{12,8},{14,10},{16,20},{18,... | collective-permute-start | bytes 1990664 | tf_op jit(solution)/shard_map/ppermute | solution.py:95
  122.1 45.3 %collective-permute-start.22 = (f32[432,384]{1,0:T(8,128)S(1)}, f32[432,384]{1,0:T(8,128)}, u32[]{:S(2)}, u32[]{:S(2)}) collective-permute-start(f32[432,384]{1,0:T(8,128)S(1)} %shard_map.364.refs_2_), channel_id=1, source_target_pairs={{0,2},{2,0},{4,6},{6,4},{8,10},{10,8},{12,14},{14,12},{16,18},{18,... | collective-permute-start | bytes 1990664 | tf_op jit(solution)/shard_map/ppermute | solution.py:95
  173.6 18.6 %collective-permute-start.31 = (f32[4,56,384]{2,1,0:T(8,128)S(1)}, f32[4,56,384]{2,1,0:T(8,128)S(1)}, u32[]{:S(2)}, u32[]{:S(2)}) collective-permute-start(f32[4,56,384]{2,1,0:T(8,128)S(1)} %get-tuple-element.175), channel_id=1, source_target_pairs={{0,2},{2,0},{4,6},{6,4},{8,10},{10,8},{12,14},{14,12},{16,18},{18,... | collective-permute-start | bytes 1032200 | tf_op jit(solution)/shard_map/ppermute | solution.py:95
  175.1 17.2 %collective-permute-start.32 = (f32[4,56,384]{2,1,0:T(8,128)S(1)}, f32[4,56,384]{2,1,0:T(8,128)S(1)}, u32[]{:S(2)}, u32[]{:S(2)}) collective-permute-start(f32[4,56,384]{2,1,0:T(8,128)S(1)} %get-tuple-element.174), channel_id=1, source_target_pairs={{0,4},{2,6},{4,0},{6,2},{8,12},{10,14},{12,8},{14,10},{16,20},{18,... | collective-permute-start | bytes 1032200 | tf_op jit(solution)/shard_map/ppermute | solution.py:95
  176.4 15.9 %collective-permute-start.33 = (f32[4,56,384]{2,1,0:T(8,128)S(1)}, f32[4,56,384]{2,1,0:T(8,128)S(1)}, u32[]{:S(2)}, u32[]{:S(2)}) collective-permute-start(f32[4,56,384]{2,1,0:T(8,128)S(1)} %get-tuple-element.173), channel_id=1, source_target_pairs={{0,6},{2,4},{4,2},{6,0},{8,14},{10,12},{12,10},{14,8},{16,22},{18,... | collective-permute-start | bytes 1032200 | tf_op jit(solution)/shard_map/ppermute | solution.py:95
  177.2 7.0 %collective-permute-start.27 = (f32[96,384]{1,0:T(8,128)S(1)}, f32[96,384]{1,0:T(8,128)S(1)}, u32[]{:S(2)}, u32[]{:S(2)}) collective-permute-start(f32[96,384]{1,0:T(8,128)S(1)} %get-tuple-element.183), channel_id=1, source_target_pairs={{0,8},{2,10},{4,12},{6,14},{8,0},{10,2},{12,4},{14,6},{16,24},{18,... | collective-permute-start | bytes 442376 | tf_op jit(solution)/shard_map/ppermute | solution.py:95
  179.1 13.1 %collective-permute-start.28 = (f32[96,384]{1,0:T(8,128)S(1)}, f32[96,384]{1,0:T(8,128)S(1)}, u32[]{:S(2)}, u32[]{:S(2)}) collective-permute-start(f32[96,384]{1,0:T(8,128)S(1)} %get-tuple-element.182), channel_id=1, source_target_pairs={{0,16},{2,18},{4,20},{6,22},{8,24},{10,26},{12,28},{14,30},{16,0},... | collective-permute-start | bytes 442376 | tf_op jit(solution)/shard_map/ppermute | solution.py:95
  184.2 8.0 %collective-permute-start.29 = (f32[96,384]{1,0:T(8,128)S(1)}, f32[96,384]{1,0:T(8,128)S(1)}, u32[]{:S(2)}, u32[]{:S(2)}) collective-permute-start(f32[96,384]{1,0:T(8,128)S(1)} %get-tuple-element.181), channel_id=1, source_target_pairs={{0,24},{2,26},{4,28},{6,30},{8,16},{10,18},{12,20},{14,22},{16,8},... | collective-permute-start | bytes 442376 | tf_op jit(solution)/shard_map/ppermute | solution.py:95
  192.5 8.3 %collective-permute-start.37 = (f32[6,197,384]{2,1,0:T(8,128)S(1)}, f32[6,197,384]{2,1,0:T(8,128)}, u32[]{:S(2)}, u32[]{:S(2)}) collective-permute-start(f32[6,197,384]{2,1,0:T(8,128)S(1)} %get-tuple-element.138), channel_id=1, source_target_pairs={{0,1},{1,0},{2,3},{3,2},{4,5},{5,4},{6,7},{7,6},{8,9},{9,8},{10,11... | collective-permute-start | bytes 5446664 | tf_op jit(solution)/shard_map/ppermute | solution.py:99
  193.0 13.7 %collective-permute-start.34 = (f32[152,384]{1,0:T(8,128)S(1)}, f32[152,384]{1,0:T(8,128)S(1)}, u32[]{:S(2)}, u32[]{:S(2)}) collective-permute-start(f32[152,384]{1,0:T(8,128)S(1)} %get-tuple-element.178), channel_id=1, source_target_pairs={{0,8},{2,10},{4,12},{6,14},{8,0},{10,2},{12,4},{14,6},{16,24},{18,... | collective-permute-start | bytes 700424 | tf_op jit(solution)/shard_map/ppermute | solution.py:95
  195.7 19.5 %collective-permute-start.35 = (f32[152,384]{1,0:T(8,128)S(1)}, f32[152,384]{1,0:T(8,128)S(1)}, u32[]{:S(2)}, u32[]{:S(2)}) collective-permute-start(f32[152,384]{1,0:T(8,128)S(1)} %get-tuple-element.177), channel_id=1, source_target_pairs={{0,16},{2,18},{4,20},{6,22},{8,24},{10,26},{12,28},{14,30},{16,0},... | collective-permute-start | bytes 700424 | tf_op jit(solution)/shard_map/ppermute | solution.py:95
  196.6 18.6 %collective-permute-start.36 = (f32[152,384]{1,0:T(8,128)S(1)}, f32[152,384]{1,0:T(8,128)S(1)}, u32[]{:S(2)}, u32[]{:S(2)}) collective-permute-start(f32[152,384]{1,0:T(8,128)S(1)} %get-tuple-element.176), channel_id=1, source_target_pairs={{0,24},{2,26},{4,28},{6,30},{8,16},{10,18},{12,20},{14,22},{16,8},... | collective-permute-start | bytes 700424 | tf_op jit(solution)/shard_map/ppermute | solution.py:95
  218.1 14.5 %collective-permute-start.40 = (f32[192,384]{1,0:T(8,128)S(1)}, f32[192,384]{1,0:T(8,128)S(1)}, u32[]{:S(2)}, u32[]{:S(2)}) collective-permute-start(f32[192,384]{1,0:T(8,128)S(1)} %dynamic-slice_add_fusion.refs_0_), channel_id=1, source_target_pairs={{0,2},{2,0},{4,6},{6,4},{8,10},{10,8},{12,14},{14,12},{16,18},{18,... | collective-permute-start | bytes 884744 | tf_op jit(solution)/shard_map/ppermute | solution.py:95
  219.6 7.1 %collective-permute-start.41 = (f32[48,384]{1,0:T(8,128)S(1)}, f32[48,384]{1,0:T(8,128)S(1)}, u32[]{:S(2)}, u32[]{:S(2)}) collective-permute-start(f32[48,384]{1,0:T(8,128)S(1)} %get-tuple-element.143.refs_2_), channel_id=1, source_target_pairs={{0,8},{2,10},{4,12},{6,14},{8,0},{10,2},{12,4},{14,6},{16,24},{18,... | collective-permute-start | bytes 221192 | tf_op jit(solution)/shard_map/ppermute | solution.py:95
  224.0 8.6 %collective-permute-start.42 = (f32[48,384]{1,0:T(8,128)S(1)}, f32[48,384]{1,0:T(8,128)S(1)}, u32[]{:S(2)}, u32[]{:S(2)}) collective-permute-start(f32[48,384]{1,0:T(8,128)S(1)} %get-tuple-element.143.refs_2_), channel_id=1, source_target_pairs={{0,16},{2,18},{4,20},{6,22},{8,24},{10,26},{12,28},{14,30},{16,0},... | collective-permute-start | bytes 221192 | tf_op jit(solution)/shard_map/ppermute | solution.py:95
  224.8 7.8 %collective-permute-start.43 = (f32[48,384]{1,0:T(8,128)S(1)}, f32[48,384]{1,0:T(8,128)S(1)}, u32[]{:S(2)}, u32[]{:S(2)}) collective-permute-start(f32[48,384]{1,0:T(8,128)S(1)} %get-tuple-element.143.refs_2_), channel_id=1, source_target_pairs={{0,24},{2,26},{4,28},{6,30},{8,16},{10,18},{12,20},{14,22},{16,8},... | collective-permute-start | bytes 221192 | tf_op jit(solution)/shard_map/ppermute | solution.py:95
  248.5 6.3 %collective-permute-start.48 = (f32[24,1152]{1,0:T(8,128)S(1)}, f32[24,1152]{1,0:T(8,128)S(1)}, u32[]{:S(2)}, u32[]{:S(2)}) collective-permute-start(f32[24,1152]{1,0:T(8,128)S(1)} %get-tuple-element.185), channel_id=1, source_target_pairs={{0,4},{2,6},{4,0},{6,2},{8,12},{10,14},{12,8},{14,10},{16,20},{18,... | collective-permute-start | bytes 331784 | tf_op jit(solution)/shard_map/ppermute | solution.py:95
  250.1 6.3 %collective-permute-start.49 = (f32[24,1152]{1,0:T(8,128)S(1)}, f32[24,1152]{1,0:T(8,128)S(1)}, u32[]{:S(2)}, u32[]{:S(2)}) collective-permute-start(f32[24,1152]{1,0:T(8,128)S(1)} %get-tuple-element.184), channel_id=1, source_target_pairs={{0,6},{2,4},{4,2},{6,0},{8,14},{10,12},{12,10},{14,8},{16,22},{18,... | collective-permute-start | bytes 331784 | tf_op jit(solution)/shard_map/ppermute | solution.py:95
  (50 other events, 351.5 us)
where the time goes:
time: 259 us; the launch traced here: 258 us
  Pallas kernels  130 us (50%)
  waiting for transfers between devices  54.9 us (21%)
  starting transfers between devices  51.8 us (20%)
  other arithmetic  11.6 us (4%)
  local copies, waits for them, and re-layouts  7.43 us (3%)
    ppermute x31, starting transfers between devices, swap_dp(): return lax.ppermute(value, 'dp', [(i, i ^ mask) for i in range(dp_size)])  47.8 us
    pallas_call x1, Pallas kernels, body(): call(functools.partial(mlp, dp_size), groups, [per_group((PAD, D)), per_g...  47.6 us
    pallas_call x1, Pallas kernels, backward(): call(functools.partial(attention_backward, dp_size, last, groups, first),...  43.9 us
    ppermute x31, waiting for transfers between devices, swap_dp(): return lax.ppermute(value, 'dp', [(i, i ^ mask) for i in range(dp_size)])  42.4 us
    pallas_call x1, Pallas kernels, body(): call(functools.partial(attention_forward, dp_size), groups, [half_images(...  23.2 us
    pallas_call x12, Pallas kernels, gated(): pl.pallas_call(run, grid=(1,), in_specs=in_specs + [anywhere] * (len(pass...  14.9 us
    ppermute x19, waiting for transfers between devices, swap_tp(): return lax.ppermute(value, 'tp', [(0, 1), (1, 0)])  12.5 us
    unnamed x69, local copies, waits for them, and re-layouts  5.21 us
  transfers between devices with their start and end apart: 50, of which 23 were waited for; matrix products, arithmetic and copies ran while one was open for 5% of the time, Pallas kernels for 26%

commit v1 on v0

--- a/solution.py
+++ b/solution.py
@@ -295,7 +295,7 @@
         )
         return carry
 
-    lax.fori_loop(0, GROUP * HEADS // 2, head_pair, 0, unroll=UNROLL)
+    lax.fori_loop(0, GROUP * HEADS // 2, head_pair, 0, unroll=True)
     attended = att[...]
     att_out[...] = attended.reshape(GROUP, PAD, D)
     hidden = tokens + nt_wide(attended, wo[: 2 * D]) + vec[0:1, 6 * D : 7 * D]
@@ -466,7 +466,7 @@
         dqkv[part, at(0)] = turned.T[:PAD] * 0.125
         return carry
 
-    lax.fori_loop(0, GROUP * HEADS // 2, head_pair, 0, unroll=UNROLL)
+    lax.fori_loop(0, GROUP * HEADS // 2, head_pair, 0, unroll=True)
     dall = dqkv[...]
     grads[...] += dot_one(rows_left(normed), rows_right(dall), 0, 0)
     dnormed = nt_wide(dall, wqkv[...])
@@ -603,11 +603,18 @@
             left, right = left_three(gram), weights_three(gram)
             mixing = ns_first * ident + ns_second * gram + ns_third * dot_one(left, right, 1, 0)
             mixing_right = weights_three(mixing)
-            total = mixing if total is None else dot_one(left_three(total), mixing_right, 1, 0)
+            if total is None:
+                total = mixing
+                inner = dot_one(left, mixing_right, 1, 0)
+            elif sweep < NS_STEPS - 1:
+                both = dot_one(lines(left, left_three(total)), mixing_right, 1, 0)
+                inner, total = both[: gram.shape[0]], both[gram.shape[0] :]
+            else:
+                total = dot_one(left_three(total[: out.shape[0]]), mixing_right, 1, 0)
             if sweep < NS_STEPS - 1:
-                gram = dot_one(left_three(dot_one(left, mixing_right, 1, 0)), mixing_right, 1, 0)
+                gram = dot_one(left_three(inner), mixing_right, 1, 0)
         factor = jnp.where(info[3] >= 2, -2.0, -1.0).astype(f32) * matrix_rate
-        out[...] = total[: out.shape[0]] * (scale * factor)
+        out[...] = total * (scale * factor)
 
     @pl.when(info[0] != 0)
     def _():
@@ -980,11 +987,12 @@
         [shaped(*small), shaped(*small)],
         [(1, VEC)],
     )
-    total_a, held_wide, held_small, send_b = gated(
+    (send_b,) = gated(pass_on, [], [], [send_b], after=plane_a)
+    total_a, held_wide, held_small = gated(
         functools.partial(close_plane, SLOTS, above, pitch),
         [info, sum_a[0]] + plane_a,
         [shaped(above, SLOTS * pitch, D), shaped(SLOTS * pitch, D), shaped(2 * pitch, D)],
-        [send_b],
+        [],
     )
     sum_b = (keep_b + swap_tp(send_b)).reshape((SLOTS, above) + small[2:])
     plane_b = [swap_dp(sum_b[s], s, dp_size) for s in range(1, plane[1])]

time: 259 us -> 256 us (0.988)
    unnamed x69 -> x75, local copies, waits for them, and re-layouts: 5.21 us -> 4.19 us
    pallas_call x12 -> x13, Pallas kernels: 14.9 us -> 14.7 us  [gated(): pl.pallas_call(run, grid=(1,), in_specs=in_specs + [anywhere] * (len(pass...]
  transfers between devices with their start and end apart: 50 -> 50, of which waited for: 23 -> 24; matrix products, arithmetic and copies ran while one was open for 5% -> 5% of each run, Pallas kernels for 26% -> 26%
where the time goes in v1:
time: 256 us; the launch traced here: 255 us
  Pallas kernels  128 us (50%)
  waiting for transfers between devices  55.4 us (22%)
  starting transfers between devices  52 us (20%)
  other arithmetic  11.6 us (5%)
  local copies, waits for them, and re-layouts  6.41 us (3%)
    pallas_call x1, Pallas kernels, body(): call(functools.partial(mlp, dp_size), groups, [per_group((PAD, D)), per_g...  47.9 us
    ppermute x31, starting transfers between devices, swap_dp(): return lax.ppermute(value, 'dp', [(i, i ^ mask) for i in range(dp_size)])  47.9 us
    ppermute x31, waiting for transfers between devices, swap_dp(): return lax.ppermute(value, 'dp', [(i, i ^ mask) for i in range(dp_size)])  44.1 us
    pallas_call x1, Pallas kernels, backward(): call(functools.partial(attention_backward, dp_size, last, groups, first),...  43.1 us
    pallas_call x1, Pallas kernels, body(): call(functools.partial(attention_forward, dp_size), groups, [half_images(...  21.2 us
    pallas_call x13, Pallas kernels, gated(): pl.pallas_call(run, grid=(1,), in_specs=in_specs + [anywhere] * (len(pass...  14.7 us
    ppermute x19, waiting for transfers between devices, swap_tp(): return lax.ppermute(value, 'tp', [(0, 1), (1, 0)])  11.4 us
  transfers between devices with their start and end apart: 50, of which 24 were waited for; matrix products, arithmetic and copies ran while one was open for 5% of the time, Pallas kernels for 26%

profile of v1, /device:TPU:0, one launch (start us, length us, event | category | flops | bytes accessed | tf_op | source)
XLA Modules:
  0.0 255.2 jit_solution(7703113531995783716)
XLA Ops:
  2.3 3.1 %collective-permute-start = (f32[1,24,896]{2,1,0:T(8,128)S(1)}, f32[1,24,896]{2,1,0:T(8,128)S(1)}, u32[]{:S(2)}, u32[]{:S(2)}) collective-permute-start(f32[1,24,896]{2,1,0:T(8,128)S(1)} %bitcast.55), channel_id=1, source_target_pairs={{0,8},{2,10},{4,12},{6,14},{8,0},{10,2},{12,4},{14,6},{16,24},{18,... | collective-permute-start | bytes 258056 | tf_op jit(solution)/shard_map/ppermute | solution.py:95
  5.4 2.6 %collective-permute-start.1 = (f32[1,24,896]{2,1,0:T(8,128)S(1)}, f32[1,24,896]{2,1,0:T(8,128)S(1)}, u32[]{:S(2)}, u32[]{:S(2)}) collective-permute-start(f32[1,24,896]{2,1,0:T(8,128)S(1)} %bitcast.56), channel_id=1, source_target_pairs={{0,16},{2,18},{4,20},{6,22},{8,24},{10,26},{12,28},{14,30},{16,0},... | collective-permute-start | bytes 258056 | tf_op jit(solution)/shard_map/ppermute | solution.py:95
  10.4 4.5 %collective-permute-done.1 = f32[1,24,896]{2,1,0:T(8,128)S(1)} collective-permute-done((f32[1,24,896]{2,1,0:T(8,128)S(1)}, f32[1,24,896]{2,1,0:T(8,128)S(1)}, u32[]{:S(2)}, u32[]{:S(2)}) %collective-permute-start.1) | collective-permute-done | bytes 86048 | tf_op jit(solution)/shard_map/ppermute | solution.py:95
  14.9 1.6 collective-permute-start.3
  20.0 1.6 collective-permute-start.7
  21.6 2.6 %collective-permute-done.6 = f32[1,24,1536]{2,1,0:T(8,128)S(1)} collective-permute-done((f32[1,24,1536]{2,1,0:T(8,128)S(1)}, f32[1,24,1536]{2,1,0:T(8,128)S(1)}, u32[]{:S(2)}, u32[]{:S(2)}) %collective-permute-start.6) | collective-permute-done | bytes 147488 | tf_op jit(solution)/shard_map/ppermute | solution.py:95
  24.1 3.2 %collective-permute-start.8 = (f32[1,24,1536]{2,1,0:T(8,128)S(1)}, f32[1,24,1536]{2,1,0:T(8,128)S(1)}, u32[]{:S(2)}, u32[]{:S(2)}) collective-permute-start(f32[1,24,1536]{2,1,0:T(8,128)S(1)} %maximum_bitcast_fusion), channel_id=1, source_target_pairs={{0,24},{2,26},{4,28},{6,30},{8,16},{10,18},{12,20},{14,22},{16,8},... | collective-permute-start | bytes 442376 | tf_op jit(solution)/shard_map/ppermute | solution.py:95
  28.6 3.7 %collective-permute-done.7 = f32[1,24,1536]{2,1,0:T(8,128)S(1)} collective-permute-done((f32[1,24,1536]{2,1,0:T(8,128)S(1)}, f32[1,24,1536]{2,1,0:T(8,128)S(1)}, u32[]{:S(2)}, u32[]{:S(2)}) %collective-permute-start.7) | collective-permute-done | bytes 147488 | tf_op jit(solution)/shard_map/ppermute | solution.py:95
  33.5 1.6 collective-permute-start.10
  38.0 21.2 %shard_map.361 = (f32[6,208,1152]{2,1,0:T(8,128)}, f32[6,208,384]{2,1,0:T(8,128)}, f32[6,208,384]{2,1,0:T(8,128)}, bf16[1152,1152]{1,0:T(8,128)(2,1)}, bf16[1152,384]{1,0:T(8,128)(2,1)}, /*index=5*/f32[1,4608]{1,0:T(1,128)}) custom-call(s32[4]{0:T(128)} %pad_add_fusion.info.refs_0_, f32[12,197,384]{2,1,0:T(8,128)} %images.3, f32[4,24,896]{2,1,0:T(8,128)} %copy-done.15, ...), custom_call_target="tpu_custom_call" | custom-call | flops 16000000000 | bytes 20971520 | tf_op jit(solution)/shard_map/pallas_call | solution.py:859
  59.3 2.2 collective-permute-done.10.rest_2_
  67.5 47.9 %shard_map.362 = (f32[6,197,384]{2,1,0:T(8,128)}, f32[6,208,384]{2,1,0:T(8,128)}, f32[6,208,384]{2,1,0:T(8,128)}, f32[4,96,384]{2,1,0:T(8,128)}, f32[4,96,384]{2...) custom-call(s32[4]{0:T(128)} %pad_add_fusion.info.refs_0_, ...), custom_call_target="tpu_custom_call" | custom-call | flops 48000000000 | bytes 20971520 | tf_op jit(solution)/shard_map/pallas_call | solution.py:897
  118.8 2.3 collective-permute-start.26
  124.2 43.1 %shard_map.369 = (f32[6,197,384]{2,1,0:T(8,128)}, f32[4,4,56,384]{3,2,1,0:T(8,128)}, f32[4,4,56,384]{3,2,1,0:T(8,128)}) custom-call(s32[4]{0:T(128)} %pad_add_fusion.info.refs_0_, f32[12,197,384]{2,1,0:T(8,128)} %images.3, f32[6,208,1152]{2,1,0:T(8,128)} %get-tuple-element.124.qkv, f32[6,208,384]{2,1,0:T(8,128)} %get-tuple-element.125.datt, ...), custom_call_target="tpu_custom_call" | custom-call | flops 30000001024 | bytes 20971520 | tf_op jit(solution)/shard_map/pallas_call | solution.py:958
  168.7 2.0 collective-permute-done.30
  171.0 1.6 collective-permute-start.31
  174.6 2.0 collective-permute-start.27
  177.6 4.1 %collective-permute-done.27.refs_1_ = f32[96,384]{1,0:T(8,128)S(1)} collective-permute-done((f32[96,384]{1,0:T(8,128)S(1)}, f32[96,384]{1,0:T(8,128)S(1)}, u32[]{:S(2)}, u32[]{:S(2)}) %collective-permute-start.27) | collective-permute-done | bytes 147488 | tf_op jit(solution)/shard_map/ppermute | solution.py:95
  181.7 1.6 collective-permute-start.29
  183.2 6.4 %collective-permute-done.28.refs_2_ = f32[96,384]{1,0:T(8,128)S(1)} collective-permute-done((f32[96,384]{1,0:T(8,128)S(1)}, f32[96,384]{1,0:T(8,128)S(1)}, u32[]{:S(2)}, u32[]{:S(2)}) %collective-permute-start.28) | collective-permute-done | bytes 147488 | tf_op jit(solution)/shard_map/ppermute | solution.py:95
  190.5 2.6 %collective-permute-start.34 = (f32[152,384]{1,0:T(8,128)S(1)}, f32[152,384]{1,0:T(8,128)S(1)}, u32[]{:S(2)}, u32[]{:S(2)}) collective-permute-start(f32[152,384]{1,0:T(8,128)S(1)} %get-tuple-element.176), channel_id=1, source_target_pairs={{0,8},{2,10},{4,12},{6,14},{8,0},{10,2},{12,4},{14,6},{16,24},{18,... | collective-permute-start | bytes 700424 | tf_op jit(solution)/shard_map/ppermute | solution.py:95
  195.9 2.3 broadcast_select_fusion.1
  198.2 1.7 broadcast_select_fusion.3
  200.0 2.1 pad_maximum_fusion.1.refs_6_
  202.1 2.1 pad_maximum_fusion.refs_5_
  204.2 8.5 %collective-permute-done.35.refs_2_ = f32[152,384]{1,0:T(8,128)S(1)} collective-permute-done((f32[152,384]{1,0:T(8,128)S(1)}, f32[152,384]{1,0:T(8,128)S(1)}, u32[]{:S(2)}, u32[]{:S(2)}) %collective-permute-start.35) | collective-permute-done | bytes 233504 | tf_op jit(solution)/shard_map/ppermute | solution.py:95
  213.5 2.0 collective-permute-done.39
  217.1 4.4 %collective-permute-start.41 = (f32[48,384]{1,0:T(8,128)S(1)}, f32[48,384]{1,0:T(8,128)S(1)}, u32[]{:S(2)}, u32[]{:S(2)}) collective-permute-start(f32[48,384]{1,0:T(8,128)S(1)} %get-tuple-element.141.refs_2_), channel_id=1, source_target_pairs={{0,8},{2,10},{4,12},{6,14},{8,0},{10,2},{12,4},{14,6},{16,24},{18,... | collective-permute-start | bytes 221192 | tf_op jit(solution)/shard_map/ppermute | solution.py:95
  224.2 5.9 %collective-permute-done.42.refs_4_ = f32[48,384]{1,0:T(8,128)S(1)} collective-permute-done((f32[48,384]{1,0:T(8,128)S(1)}, f32[48,384]{1,0:T(8,128)S(1)}, u32[]{:S(2)}, u32[]{:S(2)}) %collective-permute-start.42) | collective-permute-done | bytes 73760 | tf_op jit(solution)/shard_map/ppermute | solution.py:95
  232.2 10.2 %shard_map.375.refs_1_ = f32[96,384]{1,0:T(8,128)S(1)} custom-call(s32[4]{0:T(128)S(1)} %copy-done.13, f32[384,384]{1,0:T(8,128)S(1)} %pad_maximum_fusion.2.refs_1_, f32[192,384]{1,0:T(8,128)S(1)} %get-tuple-element.143.refs_2_, f32[192,384]{1,0:T(8,128)S(1)} %collective-permute-done.45.refs_3_), custom_call_target="tpu_custom_call" | custom-call | flops 12000000000 | bytes 1048576 | tf_op jit(solution)/shard_map/pallas_call | solution.py:779
  249.0 1.8 collective-permute-done.47.refs_2_
  251.8 1.6 collective-permute-done.49.refs_4_
  (187 shorter events, 49.0 us)
Async XLA Ops:
  2.3 8.1 %collective-permute-start = (f32[1,24,896]{2,1,0:T(8,128)S(1)}, f32[1,24,896]{2,1,0:T(8,128)S(1)}, u32[]{:S(2)}, u32[]{:S(2)}) collective-permute-start(f32[1,24,896]{2,1,0:T(8,128)S(1)} %bitcast.55), channel_id=1, source_target_pairs={{0,8},{2,10},{4,12},{6,14},{8,0},{10,2},{12,4},{14,6},{16,24},{18,... | collective-permute-start | bytes 258056 | tf_op jit(solution)/shard_map/ppermute | solution.py:95
  5.4 9.5 %collective-permute-start.1 = (f32[1,24,896]{2,1,0:T(8,128)S(1)}, f32[1,24,896]{2,1,0:T(8,128)S(1)}, u32[]{:S(2)}, u32[]{:S(2)}) collective-permute-start(f32[1,24,896]{2,1,0:T(8,128)S(1)} %bitcast.56), channel_id=1, source_target_pairs={{0,16},{2,18},{4,20},{6,22},{8,24},{10,26},{12,28},{14,30},{16,0},... | collective-permute-start | bytes 258056 | tf_op jit(solution)/shard_map/ppermute | solution.py:95
  8.0 6.9 %collective-permute-start.2 = (f32[1,24,896]{2,1,0:T(8,128)S(1)}, f32[1,24,896]{2,1,0:T(8,128)S(1)}, u32[]{:S(2)}, u32[]{:S(2)}) collective-permute-start(f32[1,24,896]{2,1,0:T(8,128)S(1)} %bitcast.57), channel_id=1, source_target_pairs={{0,24},{2,26},{4,28},{6,30},{8,16},{10,18},{12,20},{14,22},{16,8},... | collective-permute-start | bytes 258056 | tf_op jit(solution)/shard_map/ppermute | solution.py:95
  14.9 17.4 %collective-permute-start.3 = (f32[4,24,896]{2,1,0:T(8,128)S(1)}, f32[4,24,896]{2,1,0:T(8,128)S(1)}, u32[]{:S(2)}, u32[]{:S(2)}) collective-permute-start(f32[4,24,896]{2,1,0:T(8,128)S(1)} %pad_maximum_fusion.3.rest_0_), channel_id=1, source_target_pairs={{0,2},{2,0},{4,6},{6,4},{8,10},{10,8},{12,14},{14,12},{16,18},{18,... | collective-permute-start | bytes 1032200 | tf_op jit(solution)/shard_map/ppermute | solution.py:95
  16.5 15.8 %collective-permute-start.4 = (f32[4,24,896]{2,1,0:T(8,128)S(1)}, f32[4,24,896]{2,1,0:T(8,128)S(1)}, u32[]{:S(2)}, u32[]{:S(2)}) collective-permute-start(f32[4,24,896]{2,1,0:T(8,128)S(1)} %pad_maximum_fusion.3.rest_0_), channel_id=1, source_target_pairs={{0,4},{2,6},{4,0},{6,2},{8,12},{10,14},{12,8},{14,10},{16,20},{18,... | collective-permute-start | bytes 1032200 | tf_op jit(solution)/shard_map/ppermute | solution.py:95
  18.0 14.3 %collective-permute-start.5 = (f32[4,24,896]{2,1,0:T(8,128)S(1)}, f32[4,24,896]{2,1,0:T(8,128)}, u32[]{:S(2)}, u32[]{:S(2)}) collective-permute-start(f32[4,24,896]{2,1,0:T(8,128)S(1)} %pad_maximum_fusion.3.rest_0_), channel_id=1, source_target_pairs={{0,6},{2,4},{4,2},{6,0},{8,14},{10,12},{12,10},{14,8},{16,22},{18,... | collective-permute-start | bytes 1032200 | tf_op jit(solution)/shard_map/ppermute | solution.py:95
  20.0 12.2 %collective-permute-start.7 = (f32[1,24,1536]{2,1,0:T(8,128)S(1)}, f32[1,24,1536]{2,1,0:T(8,128)S(1)}, u32[]{:S(2)}, u32[]{:S(2)}) collective-permute-start(f32[1,24,1536]{2,1,0:T(8,128)S(1)} %maximum_bitcast_fusion), channel_id=1, source_target_pairs={{0,16},{2,18},{4,20},{6,22},{8,24},{10,26},{12,28},{14,30},{16,0},... | collective-permute-start | bytes 442376 | tf_op jit(solution)/shard_map/ppermute | solution.py:95
  24.1 8.1 %collective-permute-start.8 = (f32[1,24,1536]{2,1,0:T(8,128)S(1)}, f32[1,24,1536]{2,1,0:T(8,128)S(1)}, u32[]{:S(2)}, u32[]{:S(2)}) collective-permute-start(f32[1,24,1536]{2,1,0:T(8,128)S(1)} %maximum_bitcast_fusion), channel_id=1, source_target_pairs={{0,24},{2,26},{4,28},{6,30},{8,16},{10,18},{12,20},{14,22},{16,8},... | collective-permute-start | bytes 442376 | tf_op jit(solution)/shard_map/ppermute | solution.py:95
  33.5 28.0 %collective-permute-start.10 = (f32[4,24,1536]{2,1,0:T(8,128)S(1)}, f32[4,24,1536]{2,1,0:T(8,128)S(1)}, u32[]{:S(2)}, u32[]{:S(2)}) collective-permute-start(f32[4,24,1536]{2,1,0:T(8,128)S(1)} %constant_dynamic-update-slice_fusion.rest_0_), channel_id=1, source_target_pairs={{0,4},{2,6},{4,0},{6,2},{8,12},{10,14},{12,8},{14,10},{16,20},{18,... | collective-permute-start | bytes 1769480 | tf_op jit(solution)/shard_map/ppermute | solution.py:95
  35.1 26.4 %collective-permute-start.11 = (f32[4,24,1536]{2,1,0:T(8,128)S(1)}, f32[4,24,1536]{2,1,0:T(8,128)S(1)}, u32[]{:S(2)}, u32[]{:S(2)}) collective-permute-start(f32[4,24,1536]{2,1,0:T(8,128)S(1)} %constant_dynamic-update-slice_fusion.rest_0_), channel_id=1, source_target_pairs={{0,6},{2,4},{4,2},{6,0},{8,14},{10,12},{12,10},{14,8},{16,22},{18,... | collective-permute-start | bytes 1769480 | tf_op jit(solution)/shard_map/ppermute | solution.py:95
  36.5 26.4 %collective-permute-start.9 = (f32[4,24,1536]{2,1,0:T(8,128)S(1)}, f32[4,24,1536]{2,1,0:T(8,128)S(1)}, u32[]{:S(2)}, u32[]{:S(2)}) collective-permute-start(f32[4,24,1536]{2,1,0:T(8,128)S(1)} %constant_dynamic-update-slice_fusion.rest_0_), channel_id=1, source_target_pairs={{0,2},{2,0},{4,6},{6,4},{8,10},{10,8},{12,14},{14,12},{16,18},{18,... | collective-permute-start | bytes 1769480 | tf_op jit(solution)/shard_map/ppermute | solution.py:95
  37.3 26.2 %collective-permute-start.16 = (f32[4,24,1536]{2,1,0:T(8,128)S(1)}, f32[4,24,1536]{2,1,0:T(8,128)S(1)}, u32[]{:S(2)}, u32[]{:S(2)}) collective-permute-start(f32[4,24,1536]{2,1,0:T(8,128)S(1)} %constant_dynamic-update-slice_fusion.rest_0_), channel_id=1, source_target_pairs={{0,1},{1,0},{2,3},{3,2},{4,5},{5,4},{6,7},{7,6},{8,9},{9,8},{10,11... | collective-permute-start | bytes 1769480 | tf_op jit(solution)/shard_map/ppermute | solution.py:99
  116.2 7.3 %collective-permute-start.20 = (f32[4,96,384]{2,1,0:T(8,128)}, f32[4,96,384]{2,1,0:T(8,128)S(1)}, u32[]{:S(2)}, u32[]{:S(2)}) collective-permute-start(f32[4,96,384]{2,1,0:T(8,128)} %get-tuple-element.111), channel_id=1, source_target_pairs={{0,1},{1,0},{2,3},{3,2},{4,5},{5,4},{6,7},{7,6},{8,9},{9,8},{10,11... | collective-permute-start | bytes 1769480 | tf_op jit(solution)/shard_map/ppermute | solution.py:99
  118.8 48.5 %collective-permute-start.26 = (f32[432,384]{1,0:T(8,128)S(1)}, f32[432,384]{1,0:T(8,128)S(1)}, u32[]{:S(2)}, u32[]{:S(2)}) collective-permute-start(f32[432,384]{1,0:T(8,128)S(1)} %shard_map.366.refs_4_), channel_id=1, source_target_pairs={{0,6},{2,4},{4,2},{6,0},{8,14},{10,12},{12,10},{14,8},{16,22},{18,... | collective-permute-start | bytes 1990664 | tf_op jit(solution)/shard_map/ppermute | solution.py:95
  121.2 46.0 %collective-permute-start.24 = (f32[432,384]{1,0:T(8,128)S(1)}, f32[432,384]{1,0:T(8,128)S(1)}, u32[]{:S(2)}, u32[]{:S(2)}) collective-permute-start(f32[432,384]{1,0:T(8,128)S(1)} %shard_map.365.refs_3_), channel_id=1, source_target_pairs={{0,4},{2,6},{4,0},{6,2},{8,12},{10,14},{12,8},{14,10},{16,20},{18,... | collective-permute-start | bytes 1990664 | tf_op jit(solution)/shard_map/ppermute | solution.py:95
  122.9 44.4 %collective-permute-start.22 = (f32[432,384]{1,0:T(8,128)}, f32[432,384]{1,0:T(8,128)S(1)}, u32[]{:S(2)}, u32[]{:S(2)}) collective-permute-start(f32[432,384]{1,0:T(8,128)} %shard_map.364.refs_2_), channel_id=1, source_target_pairs={{0,2},{2,0},{4,6},{6,4},{8,10},{10,8},{12,14},{14,12},{16,18},{18,... | collective-permute-start | bytes 1990664 | tf_op jit(solution)/shard_map/ppermute | solution.py:95
  171.0 18.7 %collective-permute-start.31 = (f32[4,56,384]{2,1,0:T(8,128)S(1)}, f32[4,56,384]{2,1,0:T(8,128)S(1)}, u32[]{:S(2)}, u32[]{:S(2)}) collective-permute-start(f32[4,56,384]{2,1,0:T(8,128)S(1)} %get-tuple-element.173), channel_id=1, source_target_pairs={{0,2},{2,0},{4,6},{6,4},{8,10},{10,8},{12,14},{14,12},{16,18},{18,... | collective-permute-start | bytes 1032200 | tf_op jit(solution)/shard_map/ppermute | solution.py:95
  172.5 17.2 %collective-permute-start.32 = (f32[4,56,384]{2,1,0:T(8,128)S(1)}, f32[4,56,384]{2,1,0:T(8,128)S(1)}, u32[]{:S(2)}, u32[]{:S(2)}) collective-permute-start(f32[4,56,384]{2,1,0:T(8,128)S(1)} %get-tuple-element.172), channel_id=1, source_target_pairs={{0,4},{2,6},{4,0},{6,2},{8,12},{10,14},{12,8},{14,10},{16,20},{18,... | collective-permute-start | bytes 1032200 | tf_op jit(solution)/shard_map/ppermute | solution.py:95
  173.9 15.9 %collective-permute-start.33 = (f32[4,56,384]{2,1,0:T(8,128)S(1)}, f32[4,56,384]{2,1,0:T(8,128)S(1)}, u32[]{:S(2)}, u32[]{:S(2)}) collective-permute-start(f32[4,56,384]{2,1,0:T(8,128)S(1)} %get-tuple-element.171), channel_id=1, source_target_pairs={{0,6},{2,4},{4,2},{6,0},{8,14},{10,12},{12,10},{14,8},{16,22},{18,... | collective-permute-start | bytes 1032200 | tf_op jit(solution)/shard_map/ppermute | solution.py:95
  174.6 7.1 %collective-permute-start.27 = (f32[96,384]{1,0:T(8,128)S(1)}, f32[96,384]{1,0:T(8,128)S(1)}, u32[]{:S(2)}, u32[]{:S(2)}) collective-permute-start(f32[96,384]{1,0:T(8,128)S(1)} %get-tuple-element.181), channel_id=1, source_target_pairs={{0,8},{2,10},{4,12},{6,14},{8,0},{10,2},{12,4},{14,6},{16,24},{18,... | collective-permute-start | bytes 442376 | tf_op jit(solution)/shard_map/ppermute | solution.py:95
  176.5 13.1 %collective-permute-start.28 = (f32[96,384]{1,0:T(8,128)S(1)}, f32[96,384]{1,0:T(8,128)S(1)}, u32[]{:S(2)}, u32[]{:S(2)}) collective-permute-start(f32[96,384]{1,0:T(8,128)S(1)} %get-tuple-element.180), channel_id=1, source_target_pairs={{0,16},{2,18},{4,20},{6,22},{8,24},{10,26},{12,28},{14,30},{16,0},... | collective-permute-start | bytes 442376 | tf_op jit(solution)/shard_map/ppermute | solution.py:95
  181.7 8.0 %collective-permute-start.29 = (f32[96,384]{1,0:T(8,128)S(1)}, f32[96,384]{1,0:T(8,128)S(1)}, u32[]{:S(2)}, u32[]{:S(2)}) collective-permute-start(f32[96,384]{1,0:T(8,128)S(1)} %get-tuple-element.179), channel_id=1, source_target_pairs={{0,24},{2,26},{4,28},{6,30},{8,16},{10,18},{12,20},{14,22},{16,8},... | collective-permute-start | bytes 442376 | tf_op jit(solution)/shard_map/ppermute | solution.py:95
  189.9 8.3 %collective-permute-start.37 = (f32[6,197,384]{2,1,0:T(8,128)S(1)}, f32[6,197,384]{2,1,0:T(8,128)}, u32[]{:S(2)}, u32[]{:S(2)}) collective-permute-start(f32[6,197,384]{2,1,0:T(8,128)S(1)} %get-tuple-element.136), channel_id=1, source_target_pairs={{0,1},{1,0},{2,3},{3,2},{4,5},{5,4},{6,7},{7,6},{8,9},{9,8},{10,11... | collective-permute-start | bytes 5446664 | tf_op jit(solution)/shard_map/ppermute | solution.py:99
  190.5 13.7 %collective-permute-start.34 = (f32[152,384]{1,0:T(8,128)S(1)}, f32[152,384]{1,0:T(8,128)S(1)}, u32[]{:S(2)}, u32[]{:S(2)}) collective-permute-start(f32[152,384]{1,0:T(8,128)S(1)} %get-tuple-element.176), channel_id=1, source_target_pairs={{0,8},{2,10},{4,12},{6,14},{8,0},{10,2},{12,4},{14,6},{16,24},{18,... | collective-permute-start | bytes 700424 | tf_op jit(solution)/shard_map/ppermute | solution.py:95
  193.1 19.5 %collective-permute-start.35 = (f32[152,384]{1,0:T(8,128)S(1)}, f32[152,384]{1,0:T(8,128)S(1)}, u32[]{:S(2)}, u32[]{:S(2)}) collective-permute-start(f32[152,384]{1,0:T(8,128)S(1)} %get-tuple-element.175), channel_id=1, source_target_pairs={{0,16},{2,18},{4,20},{6,22},{8,24},{10,26},{12,28},{14,30},{16,0},... | collective-permute-start | bytes 700424 | tf_op jit(solution)/shard_map/ppermute | solution.py:95
  194.0 18.6 %collective-permute-start.36 = (f32[152,384]{1,0:T(8,128)S(1)}, f32[152,384]{1,0:T(8,128)S(1)}, u32[]{:S(2)}, u32[]{:S(2)}) collective-permute-start(f32[152,384]{1,0:T(8,128)S(1)} %get-tuple-element.174), channel_id=1, source_target_pairs={{0,24},{2,26},{4,28},{6,30},{8,16},{10,18},{12,20},{14,22},{16,8},... | collective-permute-start | bytes 700424 | tf_op jit(solution)/shard_map/ppermute | solution.py:95
  215.5 14.6 %collective-permute-start.40 = (f32[192,384]{1,0:T(8,128)S(1)}, f32[192,384]{1,0:T(8,128)S(1)}, u32[]{:S(2)}, u32[]{:S(2)}) collective-permute-start(f32[192,384]{1,0:T(8,128)S(1)} %dynamic-slice_add_fusion.refs_0_), channel_id=1, source_target_pairs={{0,2},{2,0},{4,6},{6,4},{8,10},{10,8},{12,14},{14,12},{16,18},{18,... | collective-permute-start | bytes 884744 | tf_op jit(solution)/shard_map/ppermute | solution.py:95
  217.1 7.1 %collective-permute-start.41 = (f32[48,384]{1,0:T(8,128)S(1)}, f32[48,384]{1,0:T(8,128)S(1)}, u32[]{:S(2)}, u32[]{:S(2)}) collective-permute-start(f32[48,384]{1,0:T(8,128)S(1)} %get-tuple-element.141.refs_2_), channel_id=1, source_target_pairs={{0,8},{2,10},{4,12},{6,14},{8,0},{10,2},{12,4},{14,6},{16,24},{18,... | collective-permute-start | bytes 221192 | tf_op jit(solution)/shard_map/ppermute | solution.py:95
  221.5 8.6 %collective-permute-start.42 = (f32[48,384]{1,0:T(8,128)S(1)}, f32[48,384]{1,0:T(8,128)S(1)}, u32[]{:S(2)}, u32[]{:S(2)}) collective-permute-start(f32[48,384]{1,0:T(8,128)S(1)} %get-tuple-element.141.refs_2_), channel_id=1, source_target_pairs={{0,16},{2,18},{4,20},{6,22},{8,24},{10,26},{12,28},{14,30},{16,0},... | collective-permute-start | bytes 221192 | tf_op jit(solution)/shard_map/ppermute | solution.py:95
  222.4 7.7 %collective-permute-start.43 = (f32[48,384]{1,0:T(8,128)S(1)}, f32[48,384]{1,0:T(8,128)S(1)}, u32[]{:S(2)}, u32[]{:S(2)}) collective-permute-start(f32[48,384]{1,0:T(8,128)S(1)} %get-tuple-element.141.refs_2_), channel_id=1, source_target_pairs={{0,24},{2,26},{4,28},{6,30},{8,16},{10,18},{12,20},{14,22},{16,8},... | collective-permute-start | bytes 221192 | tf_op jit(solution)/shard_map/ppermute | solution.py:95
  245.5 6.2 %collective-permute-start.48 = (f32[24,1152]{1,0:T(8,128)S(1)}, f32[24,1152]{1,0:T(8,128)S(1)}, u32[]{:S(2)}, u32[]{:S(2)}) collective-permute-start(f32[24,1152]{1,0:T(8,128)S(1)} %get-tuple-element.183), channel_id=1, source_target_pairs={{0,4},{2,6},{4,0},{6,2},{8,12},{10,14},{12,8},{14,10},{16,20},{18,... | collective-permute-start | bytes 331784 | tf_op jit(solution)/shard_map/ppermute | solution.py:95
  247.0 6.4 %collective-permute-start.49 = (f32[24,1152]{1,0:T(8,128)S(1)}, f32[24,1152]{1,0:T(8,128)S(1)}, u32[]{:S(2)}, u32[]{:S(2)}) collective-permute-start(f32[24,1152]{1,0:T(8,128)S(1)} %get-tuple-element.182), channel_id=1, source_target_pairs={{0,6},{2,4},{4,2},{6,0},{8,14},{10,12},{12,10},{14,8},{16,22},{18,... | collective-permute-start | bytes 331784 | tf_op jit(solution)/shard_map/ppermute | solution.py:95
  (53 other events, 321.2 us)
